TPU v7x, 512 devices: a whole 4x8x8 slice. The times are simulated.
512 devices in a mesh: seq: 64 (over z_lo, y, x), tensor: 8 (over z_hi, core).
Axes of the slice: x: 4, y: 8, z: 8 (z_hi: 4, z_lo: 2; z = z_hi * 2 + z_lo), core: 2. Of those that a mesh axis runs over, the one named last changes fastest.
Arguments:
- queries: bfloat16 [4096, 16384], P('tensor', 'seq'), may hold values from -6 to 6
- keys: bfloat16 [4096, 16384], P('tensor', 'seq'), may hold values from -6 to 6
- values: bfloat16 [4096, 16384], P('tensor', 'seq'), may hold values from -6 to 6
- out_weight: bfloat16 [4096, 4096], P('tensor', 'seq'), may hold values from -0.25 to 0.25
- decay: float32 [4096, 16], P('tensor'), may hold values from 0.5 to 500
- residue: float32 [4096, 16], P('tensor'), may hold values from -1.5 to 1.5
- skip: float32 [4096], P('tensor'), may hold values from -1 to 1
Outputs:
- mixed: bfloat16 [4096, 16384], P('tensor', 'seq')
All inputs are finite; a program needn't handle non-finite values.
Results may differ from a plain program's by a relative error of at most 0.024.
Values may be sent and summed in bfloat16 or wider, within the bound.
No kernel may reach another device: no remote copies, remote signals or barrier semaphores. Data moves between devices by JAX's collectives and lax.ppermute only.
A program may use at most 64 MiB of HBM per device.

v0:
```python
import functools

import jax
import jax.numpy as jnp
from jax import lax
from jax.experimental import pallas as pl
from jax.experimental.pallas import tpu as pltpu
from jax.sharding import Mesh, PartitionSpec as P

MODES = 16
TOTAL = 16384
SPAN = 1024
CHUNKS = 8
STEP = SPAN // CHUNKS
WIDE = 128
BLOCK = 256
VMEM = pltpu.CompilerParams(vmem_limit_bytes=40 * 1024 * 1024)
F32 = jnp.float32
BF16 = jnp.bfloat16


def pack_kernel(q_ref, k_ref, v_ref, w_ref, out_ref):
    product = (k_ref[...].astype(F32) * v_ref[...].astype(F32)).T
    out_ref[0, 0:BLOCK, :] = product.astype(BF16)
    out_ref[0, BLOCK : 2 * BLOCK, :] = q_ref[...].astype(F32).T.astype(BF16)
    out_ref[0, 2 * BLOCK :, :] = w_ref[...].astype(F32).T.astype(BF16)


def pack(q, k, v, w):
    rows = lambda width: pl.BlockSpec((WIDE, width), lambda j: (j, 0))
    return pl.pallas_call(
        pack_kernel,
        grid=(4,),
        in_specs=[rows(BLOCK), rows(BLOCK), rows(BLOCK), rows(64)],
        out_specs=pl.BlockSpec((1, 2 * BLOCK + 64, WIDE), lambda j: (j, 0, 0)),
        out_shape=jax.ShapeDtypeStruct((4, 2 * BLOCK + 64, WIDE), BF16),
        compiler_params=VMEM,
        name="pack",
    )(q, k, v, w)


def load_product(moved_ref, p_ref):
    for j in range(4):
        p_ref[BLOCK * j : BLOCK * (j + 1), :] = moved_ref[j, 0:BLOCK, :].astype(F32)


def ends_kernel(moved_ref, rate_ref, ends_ref, sent_ref, p_ref):
    load_product(moved_ref, p_ref)
    rate = rate_ref[...]
    ratio = jnp.exp(-rate)
    ratios = [jnp.broadcast_to(ratio[m : m + 1, :], (CHUNKS, WIDE)) for m in range(MODES)]

    def step(i, states):
        p = p_ref[pl.ds(i, CHUNKS, stride=STEP), :]
        return tuple(h * r + p for h, r in zip(states, ratios))

    zero = jnp.zeros((CHUNKS, WIDE), F32)
    states = lax.fori_loop(0, STEP, step, (zero,) * MODES, unroll=8)
    for m in range(MODES):
        ends_ref[pl.ds(m, CHUNKS, stride=MODES), :] = states[m]
    over_chunk = jnp.exp(-rate * STEP)
    total = ends_ref[0:MODES, :]
    for s in range(1, CHUNKS):
        total = total * over_chunk + ends_ref[MODES * s : MODES * (s + 1), :]
    for g in range(16):
        sent_ref[g] = total


def ends_call(moved, rate):
    return pl.pallas_call(
        ends_kernel,
        out_shape=[
            jax.ShapeDtypeStruct((CHUNKS * MODES, WIDE), F32),
            jax.ShapeDtypeStruct((16, MODES, WIDE), F32),
        ],
        scratch_shapes=[pltpu.VMEM((SPAN, WIDE), F32)],
        compiler_params=VMEM,
        name="ends",
    )(moved, rate)


def scan_kernel(me_ref, moved_ref, rate_ref, amp_ref, skip_ref, ends_ref, got_ref, out_ref, p_ref, y_ref, first_ref):
    load_product(moved_ref, p_ref)
    rate = rate_ref[...]
    me = me_ref[0]
    over_span = jnp.exp(-rate * SPAN)
    over_chunk = jnp.exp(-rate * STEP)
    state = jnp.zeros((MODES, WIDE), F32)
    for g in range(16):
        state = jnp.where(g < me, state * over_span + got_ref[g], state)
    for s in range(CHUNKS):
        first_ref[MODES * s : MODES * (s + 1), :] = state
        state = state * over_chunk + ends_ref[MODES * s : MODES * (s + 1), :]
    ratio = jnp.exp(-rate)
    amp = amp_ref[...]
    spread = lambda x, m: jnp.broadcast_to(x[m : m + 1, :], (CHUNKS, WIDE))
    ratios = [spread(ratio, m) for m in range(MODES)]
    amps = [spread(amp, m) for m in range(MODES)]
    firsts = tuple(first_ref[pl.ds(m, CHUNKS, stride=MODES), :] for m in range(MODES))

    def step(i, states):
        p = p_ref[pl.ds(i, CHUNKS, stride=STEP), :]
        states = tuple(h * r + p for h, r in zip(states, ratios))
        terms = [h * a for h, a in zip(states, amps)]
        while len(terms) > 1:
            terms = [terms[n] + terms[n + 1] for n in range(0, len(terms), 2)]
        y_ref[pl.ds(i, CHUNKS, stride=STEP), :] = terms[0]
        return states

    lax.fori_loop(0, STEP, step, firsts, unroll=8)
    skip = skip_ref[...]
    for j in range(4):
        rows = slice(BLOCK * j, BLOCK * (j + 1))
        filtered = (y_ref[rows, :] + skip * p_ref[rows, :]).astype(BF16)
        gate = moved_ref[j, BLOCK : 2 * BLOCK, :].astype(F32)
        out_ref[rows, :] = (gate * filtered.astype(F32)).astype(BF16)


def scan_call(me, moved, rate, amp, skip, ends, got):
    vmem = pl.BlockSpec(memory_space=pltpu.VMEM)
    return pl.pallas_call(
        scan_kernel,
        in_specs=[pl.BlockSpec(memory_space=pltpu.SMEM)] + [vmem] * 6,
        out_shape=jax.ShapeDtypeStruct((SPAN, WIDE), BF16),
        scratch_shapes=[
            pltpu.VMEM((SPAN, WIDE), F32),
            pltpu.VMEM((SPAN, WIDE), F32),
            pltpu.VMEM((CHUNKS * MODES, WIDE), F32),
        ],
        compiler_params=VMEM,
        name="scan",
    )(me, moved, rate, amp, skip, ends, got)


def project_kernel(zh_ref, w_ref, g0_ref, g1_ref, g2_ref, g3_ref, out_ref):
    zh = zh_ref[0]
    for j in range(4):
        rows = slice(BLOCK * j, BLOCK * (j + 1))
        total = jnp.zeros((512, BLOCK), F32)
        for d, g_ref in enumerate((g0_ref, g1_ref, g2_ref, g3_ref)):
            owner = lax.rem(zh + d, 4)
            for core in range(2):
                weight = w_ref[2 * owner + core]
                total += lax.dot_general(
                    weight, g_ref[core, rows, :], (((1,), (1,)), ((), ())), preferred_element_type=F32
                )
        out_ref[j] = total.astype(BF16)


def project(zh, w, *gated):
    vmem = pl.BlockSpec(memory_space=pltpu.VMEM)
    return pl.pallas_call(
        project_kernel,
        in_specs=[pl.BlockSpec(memory_space=pltpu.SMEM)] + [vmem] * 5,
        out_shape=jax.ShapeDtypeStruct((4, 512, BLOCK), BF16),
        compiler_params=VMEM,
        name="project",
    )(zh, w, *gated)


def gather_weight(block):
    perm = []
    for zl in range(2):
        for y in range(8):
            for t in range(8):
                slot = 2 * t + y % 2
                owner = zl * 4 + y // 2
                perm.append(((zl * 8 + y) * 8 + t, slot * 8 + owner))
    block = lax.ppermute(block, ("zl", "y", "zh", "core"), perm)
    spread = jnp.broadcast_to(block[None], (16,) + block.shape)
    return lax.all_to_all(spread, ("zl", "y"), 0, 0, tiled=True).reshape(8, 512, WIDE)


def per_device(q, k, v, w, decay, residue, skip):
    x = lax.axis_index("x")
    zh = lax.axis_index("zh").reshape(1)
    me = (lax.axis_index("zl") * 8 + lax.axis_index("y")).reshape(1)
    moved = lax.all_to_all(pack(q, k, v, w), "x", 0, 0, tiled=True)
    rate = lax.dynamic_slice_in_dim(decay, x * WIDE, WIDE, 0).T / TOTAL
    amp = lax.dynamic_slice_in_dim(residue, x * WIDE, WIDE, 0).T * jnp.sqrt(2.0 * rate)
    own_skip = lax.dynamic_slice_in_dim(skip, x * WIDE, WIDE, 0)[None]
    weight = gather_weight(moved[:, 2 * BLOCK :, :].reshape(256, WIDE))
    ends, sent = ends_call(moved, rate)
    got = lax.all_to_all(sent, ("zl", "y"), 0, 0, tiled=True)
    gated = scan_call(me, moved, rate, amp, own_skip, ends, got)
    shifted = [gated] + [
        lax.ppermute(gated, "zh", [((n + d) % 4, n) for n in range(4)]) for d in (1, 2, 3)
    ]
    both = [lax.all_gather(g, "core", axis=0, tiled=False) for g in shifted]
    parts = project(zh, weight, *both)
    parts = lax.all_to_all(parts, "x", 0, 0, tiled=True)
    return jnp.sum(parts.astype(F32), axis=0).astype(BF16)


def solution(mesh):
    fine = Mesh(mesh.devices.reshape(2, 8, 4, 4, 2), ("zl", "y", "x", "zh", "core"))
    seq, tensor = ("zl", "y", "x"), ("zh", "core")
    placed = (P(tensor, seq),) * 4 + (P(tensor, None), P(tensor, None), P(tensor))
    return jax.shard_map(
        per_device, mesh=fine, in_specs=placed, out_specs=P(tensor, seq), check_vma=False
    )
```

profile of v0, /device:TPU:1, one launch (start us, length us, event | category | flops | bytes accessed | tf_op | source)
XLA Modules:
  0.0 118.7 jit_solution(7424419546523880086)
XLA Ops:
  0.0 0.0 copy-start
  0.0 1.0 copy.8.w_ref
  1.0 0.0 copy-start.1
  1.0 0.9 copy-done.1
  1.9 0.0 copy-start.2
  1.9 0.9 copy-done.2
  2.9 0.0 copy-start.3
  2.9 0.9 copy-done.3
  3.8 1.7 %pack.1 = bf16[4,576,128]{2,1,0:T(8,128)(2,1)} custom-call(bf16[512,256]{1,0:T(8,128)(2,1)S(1)} %copy-done.1, bf16[512,256]{1,0:T(8,128)(2,1)S(1)} %copy-done.2, bf16[512,256]{1,0:T(8,128)(2,1)S(1)} %copy-done.3, bf16[512,64]{1,0:T(8,128)(2,1)S(1)} %copy.8.w_ref), custom_call_target="tpu_custom_call" | custom-call | tf_op jit(solution)/shard_map/pack/pallas_call | solution.py:31
  5.5 4.8 %all-to-all-start = ((bf16[4,576,128]{2,1,0:T(8,128)(2,1)}), bf16[4,576,128]{2,1,0:T(8,128)(2,1)S(1)}, u32[]{:S(2)}, u32[]{:S(2)}) async-start(bf16[4,576,128]{2,1,0:T(8,128)(2,1)} %pack.1), calls=%async_computation | async-start | bytes 1179648 | tf_op jit(solution)/shard_map/all_to_all | solution.py:178
  10.4 0.7 multiply_bitcast_fusion
  11.1 6.6 %all-to-all-done.moved_ref = bf16[4,576,128]{2,1,0:T(8,128)(2,1)S(1)} async-done(((bf16[4,576,128]{2,1,0:T(8,128)(2,1)}), bf16[4,576,128]{2,1,0:T(8,128)(2,1)S(1)}, u32[]{:S(2)}, u32[]{:S(2)}) %all-to-all-start) | async-done | bytes 589856 | tf_op jit(solution)/shard_map/all_to_all | solution.py:178
  17.7 1.5 %ends.1 = (f32[128,128]{1,0:T(8,128)S(1)}, f32[16,16,128]{2,1,0:T(8,128)}) custom-call(bf16[4,576,128]{2,1,0:T(8,128)(2,1)S(1)} %all-to-all-done.moved_ref, f32[16,128]{1,0:T(8,128)S(1)} %get-tuple-element.10.rate_ref), custom_call_target="tpu_custom_call" | custom-call | tf_op jit(solution)/shard_map/ends/pallas_call | solution.py:70
  19.2 10.7 %all-to-all-start.2 = ((f32[16,16,128]{2,1,0:T(8,128)}), f32[16,16,128]{2,1,0:T(8,128)S(1)}, u32[]{:S(2)}, u32[]{:S(2)}) async-start(f32[16,16,128]{2,1,0:T(8,128)} %get-tuple-element.8), calls=%async_computation.2 | async-start | bytes 262144 | tf_op jit(solution)/shard_map/all_to_all | solution.py:184
  29.9 6.5 %collective-permute-start = (bf16[256,128]{1,0:T(8,128)(2,1)S(1)}, bf16[256,128]{1,0:T(8,128)(2,1)S(1)}, u32[]{:S(2)}, u32[]{:S(2)}) collective-permute-start(bf16[256,128]{1,0:T(8,128)(2,1)S(1)} %bitcast.19), channel_id=1, source_target_pairs={{0,0},{1,64},{2,128},{3,192},{4,256},{5,320},{6,384},{7,448},{32,3... | collective-permute-start | bytes 196616 | tf_op jit(solution)/shard_map/ppermute | solution.py:169
  36.4 2.4 %collective-permute-done = bf16[256,128]{1,0:T(8,128)(2,1)S(1)} collective-permute-done((bf16[256,128]{1,0:T(8,128)(2,1)S(1)}, bf16[256,128]{1,0:T(8,128)(2,1)S(1)}, u32[]{:S(2)}, u32[]{:S(2)}) %collective-permute-start) | collective-permute-done | bytes 65568 | tf_op jit(solution)/shard_map/ppermute | solution.py:169
  38.8 0.0 all-to-all-done.2.got_ref
  38.8 1.2 broadcast_in_dim.4
  40.0 14.0 %all-to-all-start.1 = ((bf16[16,256,128]{2,1,0:T(8,128)(2,1)}), bf16[16,256,128]{2,1,0:T(8,128)(2,1)S(1)}, u32[]{:S(2)}, u32[]{:S(2)}) async-start(bf16[16,256,128]{2,1,0:T(8,128)(2,1)} %broadcast_in_dim.4), calls=%async_computation.1 | async-start | bytes 2097152 | tf_op jit(solution)/shard_map/all_to_all | solution.py:171
  54.1 0.0 copy-done
  54.1 0.1 dynamic-slice_bitcast_fusion.skip_ref
  54.1 1.8 %scan.1 = bf16[1024,128]{1,0:T(8,128)(2,1)S(1)} custom-call(s32[1]{0:T(128)} %bitcast.3.me_ref, bf16[4,576,128]{2,1,0:T(8,128)(2,1)S(1)} %all-to-all-done.moved_ref, f32[16,128]{1,0:T(8,128)S(1)} %get-tuple-element.10.rate_ref, f32[16,128]{1,0:T(8,128)S(1)} %get-tuple-element.9.amp_ref, f32[1,128]{1,0:T(1,128)S(1)} %dynamic-slice_bitcast_fusion.skip_ref, ...), custom_call_target="tpu_custom_call" | custom-call | tf_op jit(solution)/shard_map/scan/pallas_call | solution.py:121
  55.9 4.7 %collective-permute-start.1 = (bf16[1024,128]{1,0:T(8,128)(2,1)S(1)}, bf16[1024,128]{1,0:T(8,128)(2,1)S(1)}, u32[]{:S(2)}, u32[]{:S(2)}) collective-permute-start(bf16[1024,128]{1,0:T(8,128)(2,1)S(1)} %scan.1), channel_id=1, source_target_pairs={{2,0},{4,2},{6,4},{0,6},{3,1},{5,3},{7,5},{1,7},{10,8},{12,10},{14... | collective-permute-start | bytes 786440 | tf_op jit(solution)/shard_map/ppermute | solution.py:187
  60.6 3.0 %collective-permute-start.2 = (bf16[1024,128]{1,0:T(8,128)(2,1)S(1)}, bf16[1024,128]{1,0:T(8,128)(2,1)S(1)}, u32[]{:S(2)}, u32[]{:S(2)}) collective-permute-start(bf16[1024,128]{1,0:T(8,128)(2,1)S(1)} %scan.1), channel_id=1, source_target_pairs={{4,0},{6,2},{0,4},{2,6},{5,1},{7,3},{1,5},{3,7},{12,8},{14,10},{8,... | collective-permute-start | bytes 786440 | tf_op jit(solution)/shard_map/ppermute | solution.py:187
  63.6 3.0 %collective-permute-start.3 = (bf16[1024,128]{1,0:T(8,128)(2,1)S(1)}, bf16[1024,128]{1,0:T(8,128)(2,1)S(1)}, u32[]{:S(2)}, u32[]{:S(2)}) collective-permute-start(bf16[1024,128]{1,0:T(8,128)(2,1)S(1)} %scan.1), channel_id=1, source_target_pairs={{6,0},{0,2},{2,4},{4,6},{7,1},{1,3},{3,5},{5,7},{14,8},{8,10},{10,... | collective-permute-start | bytes 786440 | tf_op jit(solution)/shard_map/ppermute | solution.py:187
  66.5 7.2 %all-gather = bf16[2048,128]{1,0:T(8,128)(2,1)S(1)} all-gather(bf16[1024,128]{1,0:T(8,128)(2,1)S(1)} %scan.1), channel_id=2, replica_groups=mesh['zl'=2,'y'=8,'x'=4,'zh'=4,'core'=2] {'core'}, dimensions={0}, use_global_device_ids=true | all-gather | bytes 786432 | tf_op jit(solution)/shard_map/all_gather | solution.py:189
  73.7 0.0 collective-permute-done.1
  73.7 2.2 %all-gather.1 = bf16[2048,128]{1,0:T(8,128)(2,1)S(1)} all-gather(bf16[1024,128]{1,0:T(8,128)(2,1)S(1)} %collective-permute-done.1), channel_id=3, replica_groups=mesh['zl'=2,'y'=8,'x'=4,'zh'=4,'core'=2] {'core'}, dimensions={0}, use_global_device_ids=true | all-gather | bytes 786432 | tf_op jit(solution)/shard_map/all_gather | solution.py:189
  75.9 14.8 %collective-permute-done.2 = bf16[1024,128]{1,0:T(8,128)(2,1)S(1)} collective-permute-done((bf16[1024,128]{1,0:T(8,128)(2,1)S(1)}, bf16[1024,128]{1,0:T(8,128)(2,1)S(1)}, u32[]{:S(2)}, u32[]{:S(2)}) %collective-permute-start.2) | collective-permute-done | bytes 262176 | tf_op jit(solution)/shard_map/ppermute | solution.py:187
  90.6 2.8 %all-gather.2 = bf16[2048,128]{1,0:T(8,128)(2,1)S(1)} all-gather(bf16[1024,128]{1,0:T(8,128)(2,1)S(1)} %collective-permute-done.2), channel_id=4, replica_groups=mesh['zl'=2,'y'=8,'x'=4,'zh'=4,'core'=2] {'core'}, dimensions={0}, use_global_device_ids=true | all-gather | bytes 786432 | tf_op jit(solution)/shard_map/all_gather | solution.py:189
  93.4 1.4 %collective-permute-done.3 = bf16[1024,128]{1,0:T(8,128)(2,1)S(1)} collective-permute-done((bf16[1024,128]{1,0:T(8,128)(2,1)S(1)}, bf16[1024,128]{1,0:T(8,128)(2,1)S(1)}, u32[]{:S(2)}, u32[]{:S(2)}) %collective-permute-start.3) | collective-permute-done | bytes 262176 | tf_op jit(solution)/shard_map/ppermute | solution.py:187
  94.8 3.4 %all-gather.3 = bf16[2048,128]{1,0:T(8,128)(2,1)S(1)} all-gather(bf16[1024,128]{1,0:T(8,128)(2,1)S(1)} %collective-permute-done.3), channel_id=5, replica_groups=mesh['zl'=2,'y'=8,'x'=4,'zh'=4,'core'=2] {'core'}, dimensions={0}, use_global_device_ids=true | all-gather | bytes 786432 | tf_op jit(solution)/shard_map/all_gather | solution.py:189
  98.2 0.0 all-to-all-done.1
  98.2 2.3 %project.1 = bf16[4,512,256]{2,1,0:T(8,128)(2,1)S(1)} custom-call(s32[1]{0:T(128)} %bitcast.zh_ref, bf16[8,512,128]{2,1,0:T(8,128)(2,1)S(1)} %bitcast.14, bf16[2,1024,128]{2,1,0:T(8,128)(2,1)S(1)} %bitcast.15, bf16[2,1024,128]{2,1,0:T(8,128)(2,1)S(1)} %bitcast.16, bf16[2,1024,128]{2,1,0:T(8,128)(2,1)S(1)} %bitcast.17, bf16[2,1024,128]{2,1,0:T(8,128)(2,1)S(1)} %bitcast.18), custom_call_target="tpu_custom_call" | custom-call | tf_op jit(solution)/shard_map/project/pallas_call | solution.py:152
  100.5 17.3 %all_to_all.20 = bf16[4,512,256]{2,1,0:T(8,128)(2,1)S(1)} all-to-all(bf16[4,512,256]{2,1,0:T(8,128)(2,1)S(1)} %project.1), channel_id=1, replica_groups=mesh['zl'=2,'y'=8,'x'=4,'zh'=4,'core'=2] {'x'}, dimensions={0} | all-to-all | bytes 2097152 | tf_op jit(solution)/shard_map/all_to_all | solution.py:191
  117.8 0.9 reduce_sum.12
  (1 shorter events, 0.0 us)
Async XLA Ops:
  0.0 54.1 %copy-start = (f32[512]{0:T(512)S(1)}, f32[512]{0:T(512)}, u32[]{:S(2)}) copy-start(f32[512]{0:T(512)} %param.13) | copy-start | bytes 6148
  1.0 1.0 copy-start.1
  1.9 0.9 copy-start.2
  2.9 0.9 copy-start.3
  5.5 12.1 %all-to-all-start = ((bf16[4,576,128]{2,1,0:T(8,128)(2,1)}), bf16[4,576,128]{2,1,0:T(8,128)(2,1)S(1)}, u32[]{:S(2)}, u32[]{:S(2)}) async-start(bf16[4,576,128]{2,1,0:T(8,128)(2,1)} %pack.1), calls=%async_computation | async-start | bytes 1179648 | tf_op jit(solution)/shard_map/all_to_all | solution.py:178
  19.2 19.6 %all-to-all-start.2 = ((f32[16,16,128]{2,1,0:T(8,128)}), f32[16,16,128]{2,1,0:T(8,128)S(1)}, u32[]{:S(2)}, u32[]{:S(2)}) async-start(f32[16,16,128]{2,1,0:T(8,128)} %get-tuple-element.8), calls=%async_computation.2 | async-start | bytes 262144 | tf_op jit(solution)/shard_map/all_to_all | solution.py:184
  29.9 8.9 %collective-permute-start = (bf16[256,128]{1,0:T(8,128)(2,1)S(1)}, bf16[256,128]{1,0:T(8,128)(2,1)S(1)}, u32[]{:S(2)}, u32[]{:S(2)}) collective-permute-start(bf16[256,128]{1,0:T(8,128)(2,1)S(1)} %bitcast.19), channel_id=1, source_target_pairs={{0,0},{1,64},{2,128},{3,192},{4,256},{5,320},{6,384},{7,448},{32,3... | collective-permute-start | bytes 196616 | tf_op jit(solution)/shard_map/ppermute | solution.py:169
  40.0 58.2 %all-to-all-start.1 = ((bf16[16,256,128]{2,1,0:T(8,128)(2,1)}), bf16[16,256,128]{2,1,0:T(8,128)(2,1)S(1)}, u32[]{:S(2)}, u32[]{:S(2)}) async-start(bf16[16,256,128]{2,1,0:T(8,128)(2,1)} %broadcast_in_dim.4), calls=%async_computation.1 | async-start | bytes 2097152 | tf_op jit(solution)/shard_map/all_to_all | solution.py:171
  55.9 17.8 %collective-permute-start.1 = (bf16[1024,128]{1,0:T(8,128)(2,1)S(1)}, bf16[1024,128]{1,0:T(8,128)(2,1)S(1)}, u32[]{:S(2)}, u32[]{:S(2)}) collective-permute-start(bf16[1024,128]{1,0:T(8,128)(2,1)S(1)} %scan.1), channel_id=1, source_target_pairs={{2,0},{4,2},{6,4},{0,6},{3,1},{5,3},{7,5},{1,7},{10,8},{12,10},{14... | collective-permute-start | bytes 786440 | tf_op jit(solution)/shard_map/ppermute | solution.py:187
  60.6 30.0 %collective-permute-start.2 = (bf16[1024,128]{1,0:T(8,128)(2,1)S(1)}, bf16[1024,128]{1,0:T(8,128)(2,1)S(1)}, u32[]{:S(2)}, u32[]{:S(2)}) collective-permute-start(bf16[1024,128]{1,0:T(8,128)(2,1)S(1)} %scan.1), channel_id=1, source_target_pairs={{4,0},{6,2},{0,4},{2,6},{5,1},{7,3},{1,5},{3,7},{12,8},{14,10},{8,... | collective-permute-start | bytes 786440 | tf_op jit(solution)/shard_map/ppermute | solution.py:187
  63.6 31.3 %collective-permute-start.3 = (bf16[1024,128]{1,0:T(8,128)(2,1)S(1)}, bf16[1024,128]{1,0:T(8,128)(2,1)S(1)}, u32[]{:S(2)}, u32[]{:S(2)}) collective-permute-start(bf16[1024,128]{1,0:T(8,128)(2,1)S(1)} %scan.1), channel_id=1, source_target_pairs={{6,0},{0,2},{2,4},{4,6},{7,1},{1,3},{3,5},{5,7},{14,8},{8,10},{10,... | collective-permute-start | bytes 786440 | tf_op jit(solution)/shard_map/ppermute | solution.py:187
where the time goes:
time: 120 us; the launch traced here: 119 us
  starting transfers between devices  46.7 us (39%)
  blocking collectives  32.7 us (27%)
  waiting for transfers between devices  25.1 us (21%)
  Pallas kernels  7.31 us (6%)
  local copies, waits for them, and re-layouts  5.08 us (4%)
  other arithmetic  1.62 us (1%)
    all_to_all x1, blocking collectives, per_device(): parts = lax.all_to_all(parts, 'x', 0, 0, tiled=True)  17.3 us
    ppermute x3, waiting for transfers between devices, per_device(): lax.ppermute(gated, 'zh', [((n + d) % 4, n) for n in range(4)])  16.2 us
    all_gather x4, blocking collectives, per_device(): both = [lax.all_gather(g, 'core', axis=0, tiled=False) for g in shifted]  15.5 us
    all_to_all x1, starting transfers between devices, gather_weight(): lax.all_to_all(spread, ('zl', 'y'), 0, 0, tiled=True).reshape(8, 512, WIDE)  14 us
    all_to_all x1, starting transfers between devices, per_device(): got = lax.all_to_all(sent, ('zl', 'y'), 0, 0, tiled=True)  10.7 us
    ppermute x3, starting transfers between devices, per_device(): lax.ppermute(gated, 'zh', [((n + d) % 4, n) for n in range(4)])  10.6 us
    all_to_all x1, waiting for transfers between devices, per_device(): moved = lax.all_to_all(pack(q, k, v, w), 'x', 0, 0, tiled=True)  6.56 us
    ppermute x1, starting transfers between devices, gather_weight(): block = lax.ppermute(block, ('zl', 'y', 'zh', 'core'), perm)  6.48 us
  transfers between devices with their start and end apart: 7, of which 4 were waited for; matrix products, arithmetic and copies ran while one was open for 1% of the time, Pallas kernels for 1%

commit v1 on v0

--- a/solution.py
+++ b/solution.py
@@ -1,5 +1,3 @@
-import functools
-
 import jax
 import jax.numpy as jnp
 from jax import lax
@@ -19,22 +17,33 @@
 BF16 = jnp.bfloat16
 
 
-def pack_kernel(q_ref, k_ref, v_ref, w_ref, out_ref):
-    product = (k_ref[...].astype(F32) * v_ref[...].astype(F32)).T
-    out_ref[0, 0:BLOCK, :] = product.astype(BF16)
-    out_ref[0, BLOCK : 2 * BLOCK, :] = q_ref[...].astype(F32).T.astype(BF16)
-    out_ref[0, 2 * BLOCK :, :] = w_ref[...].astype(F32).T.astype(BF16)
+def pack_kernel(q_hbm, k_hbm, v_hbm, w_hbm, out_ref, q_ref, k_ref, v_ref, w_ref, sems):
+    pairs = ((k_hbm, k_ref), (v_hbm, v_ref), (q_hbm, q_ref), (w_hbm, w_ref))
+    copies = [pltpu.make_async_copy(*pair, sems.at[n]) for n, pair in enumerate(pairs)]
+    for copy in copies:
+        copy.start()
+    copies[0].wait()
+    copies[1].wait()
+    for j in range(4):
+        rows = slice(WIDE * j, WIDE * (j + 1))
+        out_ref[j, 0:BLOCK, :] = (k_ref[rows, :] * v_ref[rows, :]).T
+    copies[2].wait()
+    for j in range(4):
+        out_ref[j, BLOCK : 2 * BLOCK, :] = q_ref[WIDE * j : WIDE * (j + 1), :].T
+    copies[3].wait()
+    for j in range(4):
+        out_ref[j, 2 * BLOCK :, :] = w_ref[:, WIDE * j : WIDE * (j + 1)]
 
 
 def pack(q, k, v, w):
-    rows = lambda width: pl.BlockSpec((WIDE, width), lambda j: (j, 0))
     return pl.pallas_call(
         pack_kernel,
-        grid=(4,),
-        in_specs=[rows(BLOCK), rows(BLOCK), rows(BLOCK), rows(64)],
-        out_specs=pl.BlockSpec((1, 2 * BLOCK + 64, WIDE), lambda j: (j, 0, 0)),
+        in_specs=[pl.BlockSpec(memory_space=pltpu.HBM)] * 4,
+        out_specs=pl.BlockSpec(memory_space=pltpu.VMEM),
         out_shape=jax.ShapeDtypeStruct((4, 2 * BLOCK + 64, WIDE), BF16),
-        compiler_params=VMEM,
+        scratch_shapes=[pltpu.VMEM((4 * WIDE, BLOCK), BF16)] * 3
+        + [pltpu.VMEM((64, 4 * WIDE), BF16), pltpu.SemaphoreType.DMA((4,))],
+        compiler_params=pltpu.CompilerParams(vmem_limit_bytes=60 * 1024 * 1024),
         name="pack",
     )(q, k, v, w)
 
@@ -113,7 +122,8 @@
         rows = slice(BLOCK * j, BLOCK * (j + 1))
         filtered = (y_ref[rows, :] + skip * p_ref[rows, :]).astype(BF16)
         gate = moved_ref[j, BLOCK : 2 * BLOCK, :].astype(F32)
-        out_ref[rows, :] = (gate * filtered.astype(F32)).astype(BF16)
+        gated = (gate * filtered.astype(F32)).astype(BF16)
+        out_ref[rows, :] = gated
 
 
 def scan_call(me, moved, rate, amp, skip, ends, got):
@@ -132,22 +142,49 @@
     )(me, moved, rate, amp, skip, ends, got)
 
 
-def project_kernel(zh_ref, w_ref, g0_ref, g1_ref, g2_ref, g3_ref, out_ref):
-    zh = zh_ref[0]
-    for j in range(4):
-        rows = slice(BLOCK * j, BLOCK * (j + 1))
-        total = jnp.zeros((512, BLOCK), F32)
-        for d, g_ref in enumerate((g0_ref, g1_ref, g2_ref, g3_ref)):
-            owner = lax.rem(zh + d, 4)
-            for core in range(2):
-                weight = w_ref[2 * owner + core]
+def copies_kernel(after_ref, own_ref, far_ref, out_ref):
+    del after_ref
+    for n in range(8):
+        out_ref[n, 0] = own_ref[...]
+        out_ref[n, 1] = far_ref[...]
+
+
+def copies_of(after, own, far):
+    vmem = pl.BlockSpec(memory_space=pltpu.VMEM)
+    return pl.pallas_call(
+        copies_kernel,
+        in_specs=[pl.BlockSpec(memory_space=pl.ANY), vmem, vmem],
+        out_shape=jax.ShapeDtypeStruct((8, 2, 256, WIDE), BF16),
+        compiler_params=VMEM,
+        name="copies",
+    )(after, own, far)
+
+
+def project_kernel(place_ref, w_ref, g0_ref, g1_ref, g2_ref, g3_ref, out_ref):
+    zh, zl = place_ref[0], place_ref[1]
+    half = SPAN // 2
+    for h in range(2):
+        for part in range(2):
+            tokens = slice(half * part, half * (part + 1))
+            total = jnp.zeros((256, half), F32)
+            for d, g_ref in enumerate((g0_ref, g1_ref, g2_ref, g3_ref)):
+                owner = lax.rem(zh + d, 4)
+                weights, values = [], []
+                for core in range(2):
+                    t = 2 * owner + core
+                    weights.append(w_ref[2 * lax.rem(t, 4) + h, lax.rem(t // 4 + zl, 2)])
+                    values.append(g_ref[core, tokens, :])
                 total += lax.dot_general(
-                    weight, g_ref[core, rows, :], (((1,), (1,)), ((), ())), preferred_element_type=F32
+                    jnp.concatenate(weights, axis=1),
+                    jnp.concatenate(values, axis=1),
+                    (((1,), (1,)), ((), ())),
+                    preferred_element_type=F32,
                 )
-        out_ref[j] = total.astype(BF16)
-
-
-def project(zh, w, *gated):
+            for j in range(2):
+                out_ref[2 * part + j, 256 * h : 256 * (h + 1), :] = total[:, BLOCK * j : BLOCK * (j + 1)].astype(BF16)
+
+
+def project(place, w, *gated):
     vmem = pl.BlockSpec(memory_space=pltpu.VMEM)
     return pl.pallas_call(
         project_kernel,
@@ -155,41 +192,57 @@
         out_shape=jax.ShapeDtypeStruct((4, 512, BLOCK), BF16),
         compiler_params=VMEM,
         name="project",
-    )(zh, w, *gated)
+    )(place, w, *gated)
+
+
+def finish_kernel(parts_ref, out_ref):
+    total = parts_ref[0].astype(F32)
+    for n in range(1, 4):
+        total += parts_ref[n].astype(F32)
+    out_ref[...] = total.astype(BF16)
+
+
+def finish(parts):
+    return pl.pallas_call(
+        finish_kernel,
+        out_shape=jax.ShapeDtypeStruct((512, BLOCK), BF16),
+        compiler_params=VMEM,
+        name="finish",
+    )(parts)
 
 
 def gather_weight(block):
-    perm = []
-    for zl in range(2):
-        for y in range(8):
-            for t in range(8):
-                slot = 2 * t + y % 2
-                owner = zl * 4 + y // 2
-                perm.append(((zl * 8 + y) * 8 + t, slot * 8 + owner))
-    block = lax.ppermute(block, ("zl", "y", "zh", "core"), perm)
-    spread = jnp.broadcast_to(block[None], (16,) + block.shape)
-    return lax.all_to_all(spread, ("zl", "y"), 0, 0, tiled=True).reshape(8, 512, WIDE)
+    out = []
+    for flip in range(2):
+        perm = []
+        for zl in range(2):
+            for y in range(8):
+                for t in range(8):
+                    place = (2 * t + y % 2 + 8 * flip) % 16
+                    perm.append(((zl * 8 + y) * 8 + t, place * 8 + zl * 4 + y // 2))
+        out.append(lax.ppermute(block, ("zl", "y", "zh", "core"), perm))
+    return out
 
 
 def per_device(q, k, v, w, decay, residue, skip):
     x = lax.axis_index("x")
-    zh = lax.axis_index("zh").reshape(1)
-    me = (lax.axis_index("zl") * 8 + lax.axis_index("y")).reshape(1)
-    moved = lax.all_to_all(pack(q, k, v, w), "x", 0, 0, tiled=True)
+    zh, zl = lax.axis_index("zh"), lax.axis_index("zl")
+    me = (zl * 8 + lax.axis_index("y")).reshape(1)
+    moved = lax.all_to_all(pack(q, k, v, w.T), "x", 0, 0, tiled=True)
     rate = lax.dynamic_slice_in_dim(decay, x * WIDE, WIDE, 0).T / TOTAL
     amp = lax.dynamic_slice_in_dim(residue, x * WIDE, WIDE, 0).T * jnp.sqrt(2.0 * rate)
     own_skip = lax.dynamic_slice_in_dim(skip, x * WIDE, WIDE, 0)[None]
-    weight = gather_weight(moved[:, 2 * BLOCK :, :].reshape(256, WIDE))
     ends, sent = ends_call(moved, rate)
     got = lax.all_to_all(sent, ("zl", "y"), 0, 0, tiled=True)
+    pieces = gather_weight(moved[:, 2 * BLOCK :, :].reshape(256, WIDE))
     gated = scan_call(me, moved, rate, amp, own_skip, ends, got)
+    weight = lax.all_to_all(copies_of(gated, *pieces), "y", 0, 0, tiled=True)
     shifted = [gated] + [
         lax.ppermute(gated, "zh", [((n + d) % 4, n) for n in range(4)]) for d in (1, 2, 3)
     ]
     both = [lax.all_gather(g, "core", axis=0, tiled=False) for g in shifted]
-    parts = project(zh, weight, *both)
-    parts = lax.all_to_all(parts, "x", 0, 0, tiled=True)
-    return jnp.sum(parts.astype(F32), axis=0).astype(BF16)
+    parts = project(jnp.stack([zh, zl]), weight, *both)
+    return finish(lax.all_to_all(parts, "x", 0, 0, tiled=True))
 
 
 def solution(mesh):

time: 120 us -> 110 us (0.917)
  waiting for transfers between devices: 25.1 us -> 18.9 us
  local copies, waits for them, and re-layouts: 5.08 us -> 0.09 us
  starting transfers between devices: 46.7 us -> 50.7 us
  blocking collectives: 32.7 us -> 29.7 us
  Pallas kernels: 7.31 us -> 9.24 us
    ppermute x1 -> x2, starting transfers between devices: 6.48 us -> 14 us  [gather_weight(): out.append(lax.ppermute(block, ('zl', 'y', 'zh', 'core'), perm))]
    ppermute x3, waiting for transfers between devices: 16.2 us -> 10 us  [per_device(): lax.ppermute(gated, 'zh', [((n + d) % 4, n) for n in range(4)])]
    all_to_all x2, starting transfers between devices: 18.9 us -> 12.8 us  [the longest x1 7.91 us: per_device(): weight = lax.all_to_all(copies_of(gated, *pieces), 'y', 0, 0, tiled=True)]
    unnamed x9 -> x2, local copies, waits for them, and re-layouts: 3.82 us -> 0.01 us
    all_gather x4, blocking collectives: 15.5 us -> 12.5 us  [per_device(): both = [lax.all_gather(g, 'core', axis=0, tiled=False) for g in shifted]]
    ppermute x3, starting transfers between devices: 10.6 us -> 13.3 us  [per_device(): lax.ppermute(gated, 'zh', [((n + d) % 4, n) for n in range(4)])]
    pallas_call x1 -> x3, Pallas kernels: 1.68 us -> 4.09 us  [the longest x1 2.15 us: pack(): pl.pallas_call(pack_kernel, in_specs=[pl.BlockSpec(memory_space=pltpu.HBM...]
  transfers between devices with their start and end apart: 7 -> 8, of which waited for: 4 -> 5; matrix products, arithmetic and copies ran while one was open for 1% -> 1% of each run, Pallas kernels for 1% -> 2%
where the time goes in v1:
time: 110 us
  starting transfers between devices  50.7 us (46%)
  blocking collectives  29.7 us (27%)
  waiting for transfers between devices  18.9 us (17%)
  Pallas kernels  9.24 us (8%)
    all_to_all x1, blocking collectives, per_device(): return finish(lax.all_to_all(parts, 'x', 0, 0, tiled=True))  17.3 us
    ppermute x2, starting transfers between devices, gather_weight(): out.append(lax.ppermute(block, ('zl', 'y', 'zh', 'core'), perm))  14 us
    ppermute x3, starting transfers between devices, per_device(): lax.ppermute(gated, 'zh', [((n + d) % 4, n) for n in range(4)])  13.3 us
    all_gather x4, blocking collectives, per_device(): both = [lax.all_gather(g, 'core', axis=0, tiled=False) for g in shifted]  12.5 us
    all_to_all x1, starting transfers between devices, per_device(): got = lax.all_to_all(sent, ('zl', 'y'), 0, 0, tiled=True)  10.7 us
    ppermute x3, waiting for transfers between devices, per_device(): lax.ppermute(gated, 'zh', [((n + d) % 4, n) for n in range(4)])  10 us
    all_to_all x1, starting transfers between devices, per_device(): weight = lax.all_to_all(copies_of(gated, *pieces), 'y', 0, 0, tiled=True)  7.91 us
    all_to_all x1, waiting for transfers between devices, per_device(): moved = lax.all_to_all(pack(q, k, v, w.T), 'x', 0, 0, tiled=True)  6.56 us
  transfers between devices with their start and end apart: 8, of which 5 were waited for; matrix products, arithmetic and copies ran while one was open for 1% of the time, Pallas kernels for 2%

profile of v1, /device:TPU:1, one launch (start us, length us, event | category | flops | bytes accessed | tf_op | source)
XLA Modules:
  0.0 109.6 jit_solution(2603454135696715544)
XLA Ops:
  0.0 0.0 copy-start
  0.0 2.1 %pack.1 = bf16[4,576,128]{2,1,0:T(8,128)(2,1)} custom-call(bf16[512,256]{1,0:T(8,128)(2,1)} %q_hbm.1, bf16[512,256]{1,0:T(8,128)(2,1)} %k_hbm.1, bf16[512,256]{1,0:T(8,128)(2,1)} %v_hbm.1, bf16[64,512]{1,0:T(8,128)(2,1)} %bitcast.19), custom_call_target="tpu_custom_call" | custom-call | tf_op jit(solution)/shard_map/pack/pallas_call | solution.py:39
  2.2 4.9 %all-to-all-start = ((bf16[4,576,128]{2,1,0:T(8,128)(2,1)}), bf16[4,576,128]{2,1,0:T(8,128)(2,1)S(1)}, u32[]{:S(2)}, u32[]{:S(2)}) async-start(bf16[4,576,128]{2,1,0:T(8,128)(2,1)} %pack.1), calls=%async_computation | async-start | bytes 1179648 | tf_op jit(solution)/shard_map/all_to_all | solution.py:231
  7.0 0.7 multiply_bitcast_fusion
  7.7 6.6 %all-to-all-done.moved_ref = bf16[4,576,128]{2,1,0:T(8,128)(2,1)S(1)} async-done(((bf16[4,576,128]{2,1,0:T(8,128)(2,1)}), bf16[4,576,128]{2,1,0:T(8,128)(2,1)S(1)}, u32[]{:S(2)}, u32[]{:S(2)}) %all-to-all-start) | async-done | bytes 589856 | tf_op jit(solution)/shard_map/all_to_all | solution.py:231
  14.3 1.5 %ends.1 = (f32[128,128]{1,0:T(8,128)S(1)}, f32[16,16,128]{2,1,0:T(8,128)}) custom-call(bf16[4,576,128]{2,1,0:T(8,128)(2,1)S(1)} %all-to-all-done.moved_ref, f32[16,128]{1,0:T(8,128)S(1)} %get-tuple-element.10.rate_ref), custom_call_target="tpu_custom_call" | custom-call | tf_op jit(solution)/shard_map/ends/pallas_call | solution.py:79
  15.8 10.7 %all-to-all-start.1 = ((f32[16,16,128]{2,1,0:T(8,128)}), f32[16,16,128]{2,1,0:T(8,128)S(1)}, u32[]{:S(2)}, u32[]{:S(2)}) async-start(f32[16,16,128]{2,1,0:T(8,128)} %get-tuple-element.8), calls=%async_computation.1 | async-start | bytes 262144 | tf_op jit(solution)/shard_map/all_to_all | solution.py:236
  26.6 6.5 %collective-permute-start = (bf16[256,128]{1,0:T(8,128)(2,1)S(1)}, bf16[256,128]{1,0:T(8,128)(2,1)S(1)}, u32[]{:S(2)}, u32[]{:S(2)}) collective-permute-start(bf16[256,128]{1,0:T(8,128)(2,1)S(1)} %bitcast.20), channel_id=1, source_target_pairs={{0,0},{1,64},{2,128},{3,192},{4,256},{5,320},{6,384},{7,448},{32,3... | collective-permute-start | bytes 196616 | tf_op jit(solution)/shard_map/ppermute | solution.py:223
  33.1 7.5 %collective-permute-start.1 = (bf16[256,128]{1,0:T(8,128)(2,1)S(1)}, bf16[256,128]{1,0:T(8,128)(2,1)S(1)}, u32[]{:S(2)}, u32[]{:S(2)}) collective-permute-start(bf16[256,128]{1,0:T(8,128)(2,1)S(1)} %bitcast.21), channel_id=1, source_target_pairs={{0,256},{1,320},{2,384},{3,448},{4,0},{5,64},{6,128},{7,192},{32,2... | collective-permute-start | bytes 196616 | tf_op jit(solution)/shard_map/ppermute | solution.py:223
  40.6 0.0 copy-done
  40.6 0.1 dynamic-slice_bitcast_fusion.skip_ref
  40.7 0.0 all-to-all-done.1.got_ref
  40.7 1.8 %scan.1.after_ref = bf16[1024,128]{1,0:T(8,128)(2,1)S(1)} custom-call(s32[1]{0:T(128)} %bitcast.2.me_ref, bf16[4,576,128]{2,1,0:T(8,128)(2,1)S(1)} %all-to-all-done.moved_ref, f32[16,128]{1,0:T(8,128)S(1)} %get-tuple-element.10.rate_ref, f32[16,128]{1,0:T(8,128)S(1)} %get-tuple-element.9.amp_ref, f32[1,128]{1,0:T(1,128)S(1)} %dynamic-slice_bitcast_fusion.skip_ref, ...), custom_call_target="tpu_custom_call" | custom-call | tf_op jit(solution)/shard_map/scan/pallas_call | solution.py:131
  42.5 0.0 collective-permute-done.own_ref
  42.5 2.3 %collective-permute-done.1.far_ref = bf16[256,128]{1,0:T(8,128)(2,1)S(1)} collective-permute-done((bf16[256,128]{1,0:T(8,128)(2,1)S(1)}, bf16[256,128]{1,0:T(8,128)(2,1)S(1)}, u32[]{:S(2)}, u32[]{:S(2)}) %collective-permute-start.1) | collective-permute-done | bytes 65568 | tf_op jit(solution)/shard_map/ppermute | solution.py:223
  44.8 1.1 %copies.1 = bf16[8,2,256,128]{3,2,1,0:T(8,128)(2,1)} custom-call(bf16[1024,128]{1,0:T(8,128)(2,1)S(1)} %scan.1.after_ref, bf16[256,128]{1,0:T(8,128)(2,1)S(1)} %collective-permute-done.own_ref, bf16[256,128]{1,0:T(8,128)(2,1)S(1)} %collective-permute-done.1.far_ref), custom_call_target="tpu_custom_call" | custom-call | tf_op jit(solution)/shard_map/copies/pallas_call | solution.py:154
  45.9 7.9 %all-to-all-start.2 = ((bf16[8,2,256,128]{3,2,1,0:T(8,128)(2,1)}), bf16[8,2,256,128]{3,2,1,0:T(8,128)(2,1)S(1)}, u32[]{:S(2)}, u32[]{:S(2)}) async-start(bf16[8,2,256,128]{3,2,1,0:T(8,128)(2,1)} %copies.1), calls=%async_computation.2 | async-start | bytes 2097152 | tf_op jit(solution)/shard_map/all_to_all | solution.py:239
  53.8 5.9 %collective-permute-start.3 = (bf16[1024,128]{1,0:T(8,128)(2,1)S(1)}, bf16[1024,128]{1,0:T(8,128)(2,1)S(1)}, u32[]{:S(2)}, u32[]{:S(2)}) collective-permute-start(bf16[1024,128]{1,0:T(8,128)(2,1)S(1)} %scan.1.after_ref), channel_id=1, source_target_pairs={{4,0},{6,2},{0,4},{2,6},{5,1},{7,3},{1,5},{3,7},{12,8},{14,10},{8,... | collective-permute-start | bytes 786440 | tf_op jit(solution)/shard_map/ppermute | solution.py:241
  59.7 0.1 pad_add_fusion.place_ref
  59.7 1.9 %collective-permute-start.4 = (bf16[1024,128]{1,0:T(8,128)(2,1)S(1)}, bf16[1024,128]{1,0:T(8,128)(2,1)S(1)}, u32[]{:S(2)}, u32[]{:S(2)}) collective-permute-start(bf16[1024,128]{1,0:T(8,128)(2,1)S(1)} %scan.1.after_ref), channel_id=1, source_target_pairs={{6,0},{0,2},{2,4},{4,6},{7,1},{1,3},{3,5},{5,7},{14,8},{8,10},{10,... | collective-permute-start | bytes 786440 | tf_op jit(solution)/shard_map/ppermute | solution.py:241
  61.7 5.5 %collective-permute-start.2 = (bf16[1024,128]{1,0:T(8,128)(2,1)S(1)}, bf16[1024,128]{1,0:T(8,128)(2,1)S(1)}, u32[]{:S(2)}, u32[]{:S(2)}) collective-permute-start(bf16[1024,128]{1,0:T(8,128)(2,1)S(1)} %scan.1.after_ref), channel_id=1, source_target_pairs={{2,0},{4,2},{6,4},{0,6},{3,1},{5,3},{7,5},{1,7},{10,8},{12,10},{14... | collective-permute-start | bytes 786440 | tf_op jit(solution)/shard_map/ppermute | solution.py:241
  67.1 4.4 %all-gather = bf16[2048,128]{1,0:T(8,128)(2,1)S(1)} all-gather(bf16[1024,128]{1,0:T(8,128)(2,1)S(1)} %scan.1.after_ref), channel_id=2, replica_groups=mesh['zl'=2,'y'=8,'x'=4,'zh'=4,'core'=2] {'core'}, dimensions={0}, use_global_device_ids=true | all-gather | bytes 786432 | tf_op jit(solution)/shard_map/all_gather | solution.py:243
  71.5 1.5 %collective-permute-done.3 = bf16[1024,128]{1,0:T(8,128)(2,1)S(1)} collective-permute-done((bf16[1024,128]{1,0:T(8,128)(2,1)S(1)}, bf16[1024,128]{1,0:T(8,128)(2,1)S(1)}, u32[]{:S(2)}, u32[]{:S(2)}) %collective-permute-start.3) | collective-permute-done | bytes 262176 | tf_op jit(solution)/shard_map/ppermute | solution.py:241
  73.0 2.8 %all-gather.2 = bf16[2048,128]{1,0:T(8,128)(2,1)S(1)} all-gather(bf16[1024,128]{1,0:T(8,128)(2,1)S(1)} %collective-permute-done.3), channel_id=4, replica_groups=mesh['zl'=2,'y'=8,'x'=4,'zh'=4,'core'=2] {'core'}, dimensions={0}, use_global_device_ids=true | all-gather | bytes 786432 | tf_op jit(solution)/shard_map/all_gather | solution.py:243
  75.8 1.7 %collective-permute-done.4 = bf16[1024,128]{1,0:T(8,128)(2,1)S(1)} collective-permute-done((bf16[1024,128]{1,0:T(8,128)(2,1)S(1)}, bf16[1024,128]{1,0:T(8,128)(2,1)S(1)}, u32[]{:S(2)}, u32[]{:S(2)}) %collective-permute-start.4) | collective-permute-done | bytes 262176 | tf_op jit(solution)/shard_map/ppermute | solution.py:241
  77.5 3.0 %all-gather.3 = bf16[2048,128]{1,0:T(8,128)(2,1)S(1)} all-gather(bf16[1024,128]{1,0:T(8,128)(2,1)S(1)} %collective-permute-done.4), channel_id=5, replica_groups=mesh['zl'=2,'y'=8,'x'=4,'zh'=4,'core'=2] {'core'}, dimensions={0}, use_global_device_ids=true | all-gather | bytes 786432 | tf_op jit(solution)/shard_map/all_gather | solution.py:243
  80.5 6.8 %collective-permute-done.2 = bf16[1024,128]{1,0:T(8,128)(2,1)S(1)} collective-permute-done((bf16[1024,128]{1,0:T(8,128)(2,1)S(1)}, bf16[1024,128]{1,0:T(8,128)(2,1)S(1)}, u32[]{:S(2)}, u32[]{:S(2)}) %collective-permute-start.2) | collective-permute-done | bytes 262176 | tf_op jit(solution)/shard_map/ppermute | solution.py:241
  87.3 2.3 %all-gather.1 = bf16[2048,128]{1,0:T(8,128)(2,1)S(1)} all-gather(bf16[1024,128]{1,0:T(8,128)(2,1)S(1)} %collective-permute-done.2), channel_id=3, replica_groups=mesh['zl'=2,'y'=8,'x'=4,'zh'=4,'core'=2] {'core'}, dimensions={0}, use_global_device_ids=true | all-gather | bytes 786432 | tf_op jit(solution)/shard_map/all_gather | solution.py:243
  89.6 0.0 all-to-all-done.2.w_ref
  89.6 1.9 %project.1 = bf16[4,512,256]{2,1,0:T(8,128)(2,1)S(1)} custom-call(s32[2]{0:T(128)S(1)} %pad_add_fusion.place_ref, bf16[8,2,256,128]{3,2,1,0:T(8,128)(2,1)S(1)} %all-to-all-done.2.w_ref, bf16[2,1024,128]{2,1,0:T(8,128)(2,1)S(1)} %bitcast.15, bf16[2,1024,128]{2,1,0:T(8,128)(2,1)S(1)} %bitcast.18, bf16[2,1024,128]{2,1,0:T(8,128)(2,1)S(1)} %bitcast.16, ...), custom_call_target="tpu_custom_call" | custom-call | tf_op jit(solution)/shard_map/project/pallas_call | solution.py:189
  91.5 17.3 %all_to_all.20.parts_ref = bf16[4,512,256]{2,1,0:T(8,128)(2,1)S(1)} all-to-all(bf16[4,512,256]{2,1,0:T(8,128)(2,1)S(1)} %project.1), channel_id=1, replica_groups=mesh['zl'=2,'y'=8,'x'=4,'zh'=4,'core'=2] {'x'}, dimensions={0} | all-to-all | bytes 2097152 | tf_op jit(solution)/shard_map/all_to_all | solution.py:245
  108.7 0.8 finish.1
  (1 shorter events, 0.0 us)
Async XLA Ops:
  0.0 40.6 %copy-start = (f32[512]{0:T(512)S(1)}, f32[512]{0:T(512)}, u32[]{:S(2)}) copy-start(f32[512]{0:T(512)} %param.13) | copy-start | bytes 6148
  2.2 12.1 %all-to-all-start = ((bf16[4,576,128]{2,1,0:T(8,128)(2,1)}), bf16[4,576,128]{2,1,0:T(8,128)(2,1)S(1)}, u32[]{:S(2)}, u32[]{:S(2)}) async-start(bf16[4,576,128]{2,1,0:T(8,128)(2,1)} %pack.1), calls=%async_computation | async-start | bytes 1179648 | tf_op jit(solution)/shard_map/all_to_all | solution.py:231
  15.8 24.9 %all-to-all-start.1 = ((f32[16,16,128]{2,1,0:T(8,128)}), f32[16,16,128]{2,1,0:T(8,128)S(1)}, u32[]{:S(2)}, u32[]{:S(2)}) async-start(f32[16,16,128]{2,1,0:T(8,128)} %get-tuple-element.8), calls=%async_computation.1 | async-start | bytes 262144 | tf_op jit(solution)/shard_map/all_to_all | solution.py:236
  26.6 15.9 %collective-permute-start = (bf16[256,128]{1,0:T(8,128)(2,1)S(1)}, bf16[256,128]{1,0:T(8,128)(2,1)S(1)}, u32[]{:S(2)}, u32[]{:S(2)}) collective-permute-start(bf16[256,128]{1,0:T(8,128)(2,1)S(1)} %bitcast.20), channel_id=1, source_target_pairs={{0,0},{1,64},{2,128},{3,192},{4,256},{5,320},{6,384},{7,448},{32,3... | collective-permute-start | bytes 196616 | tf_op jit(solution)/shard_map/ppermute | solution.py:223
  33.1 11.7 %collective-permute-start.1 = (bf16[256,128]{1,0:T(8,128)(2,1)S(1)}, bf16[256,128]{1,0:T(8,128)(2,1)S(1)}, u32[]{:S(2)}, u32[]{:S(2)}) collective-permute-start(bf16[256,128]{1,0:T(8,128)(2,1)S(1)} %bitcast.21), channel_id=1, source_target_pairs={{0,256},{1,320},{2,384},{3,448},{4,0},{5,64},{6,128},{7,192},{32,2... | collective-permute-start | bytes 196616 | tf_op jit(solution)/shard_map/ppermute | solution.py:223
  45.9 43.8 %all-to-all-start.2 = ((bf16[8,2,256,128]{3,2,1,0:T(8,128)(2,1)}), bf16[8,2,256,128]{3,2,1,0:T(8,128)(2,1)S(1)}, u32[]{:S(2)}, u32[]{:S(2)}) async-start(bf16[8,2,256,128]{3,2,1,0:T(8,128)(2,1)} %copies.1), calls=%async_computation.2 | async-start | bytes 2097152 | tf_op jit(solution)/shard_map/all_to_all | solution.py:239
  53.8 19.3 %collective-permute-start.3 = (bf16[1024,128]{1,0:T(8,128)(2,1)S(1)}, bf16[1024,128]{1,0:T(8,128)(2,1)S(1)}, u32[]{:S(2)}, u32[]{:S(2)}) collective-permute-start(bf16[1024,128]{1,0:T(8,128)(2,1)S(1)} %scan.1.after_ref), channel_id=1, source_target_pairs={{4,0},{6,2},{0,4},{2,6},{5,1},{7,3},{1,5},{3,7},{12,8},{14,10},{8,... | collective-permute-start | bytes 786440 | tf_op jit(solution)/shard_map/ppermute | solution.py:241
  59.7 17.8 %collective-permute-start.4 = (bf16[1024,128]{1,0:T(8,128)(2,1)S(1)}, bf16[1024,128]{1,0:T(8,128)(2,1)S(1)}, u32[]{:S(2)}, u32[]{:S(2)}) collective-permute-start(bf16[1024,128]{1,0:T(8,128)(2,1)S(1)} %scan.1.after_ref), channel_id=1, source_target_pairs={{6,0},{0,2},{2,4},{4,6},{7,1},{1,3},{3,5},{5,7},{14,8},{8,10},{10,... | collective-permute-start | bytes 786440 | tf_op jit(solution)/shard_map/ppermute | solution.py:241
  61.7 25.7 %collective-permute-start.2 = (bf16[1024,128]{1,0:T(8,128)(2,1)S(1)}, bf16[1024,128]{1,0:T(8,128)(2,1)S(1)}, u32[]{:S(2)}, u32[]{:S(2)}) collective-permute-start(bf16[1024,128]{1,0:T(8,128)(2,1)S(1)} %scan.1.after_ref), channel_id=1, source_target_pairs={{2,0},{4,2},{6,4},{0,6},{3,1},{5,3},{7,5},{1,7},{10,8},{12,10},{14... | collective-permute-start | bytes 786440 | tf_op jit(solution)/shard_map/ppermute | solution.py:241

commit v2 on v1

--- a/solution.py
+++ b/solution.py
@@ -142,22 +142,34 @@
     )(me, moved, rate, amp, skip, ends, got)
 
 
-def copies_kernel(after_ref, own_ref, far_ref, out_ref):
+def hold_kernel(after_ref, own_ref, out_ref):
     del after_ref
+    out_ref[...] = own_ref[...]
+
+
+def hold(after, own):
+    return pl.pallas_call(
+        hold_kernel,
+        in_specs=[pl.BlockSpec(memory_space=pl.ANY), pl.BlockSpec(memory_space=pltpu.VMEM)],
+        out_shape=jax.ShapeDtypeStruct(own.shape, BF16),
+        compiler_params=VMEM,
+        name="hold",
+    )(after, own)
+
+
+def copies_kernel(own_ref, far_ref, out_ref):
     for n in range(8):
         out_ref[n, 0] = own_ref[...]
         out_ref[n, 1] = far_ref[...]
 
 
-def copies_of(after, own, far):
-    vmem = pl.BlockSpec(memory_space=pltpu.VMEM)
+def copies_of(own, far):
     return pl.pallas_call(
         copies_kernel,
-        in_specs=[pl.BlockSpec(memory_space=pl.ANY), vmem, vmem],
         out_shape=jax.ShapeDtypeStruct((8, 2, 256, WIDE), BF16),
         compiler_params=VMEM,
         name="copies",
-    )(after, own, far)
+    )(own, far)
 
 
 def project_kernel(place_ref, w_ref, g0_ref, g1_ref, g2_ref, g3_ref, out_ref):
@@ -211,17 +223,13 @@
     )(parts)
 
 
-def gather_weight(block):
-    out = []
-    for flip in range(2):
-        perm = []
-        for zl in range(2):
-            for y in range(8):
-                for t in range(8):
-                    place = (2 * t + y % 2 + 8 * flip) % 16
-                    perm.append(((zl * 8 + y) * 8 + t, place * 8 + zl * 4 + y // 2))
-        out.append(lax.ppermute(block, ("zl", "y", "zh", "core"), perm))
-    return out
+def place_weight(block):
+    perm = []
+    for zl in range(2):
+        for y in range(8):
+            for t in range(8):
+                perm.append(((zl * 8 + y) * 8 + t, (2 * t + y % 2) * 8 + zl * 4 + y // 2))
+    return lax.ppermute(block, ("zl", "y", "zh", "core"), perm)
 
 
 def per_device(q, k, v, w, decay, residue, skip):
@@ -234,9 +242,10 @@
     own_skip = lax.dynamic_slice_in_dim(skip, x * WIDE, WIDE, 0)[None]
     ends, sent = ends_call(moved, rate)
     got = lax.all_to_all(sent, ("zl", "y"), 0, 0, tiled=True)
-    pieces = gather_weight(moved[:, 2 * BLOCK :, :].reshape(256, WIDE))
+    own = place_weight(moved[:, 2 * BLOCK :, :].reshape(256, WIDE))
     gated = scan_call(me, moved, rate, amp, own_skip, ends, got)
-    weight = lax.all_to_all(copies_of(gated, *pieces), "y", 0, 0, tiled=True)
+    far = lax.ppermute(hold(gated, own), "zl", [(0, 1), (1, 0)])
+    weight = lax.all_to_all(copies_of(own, far), "y", 0, 0, tiled=True)
     shifted = [gated] + [
         lax.ppermute(gated, "zh", [((n + d) % 4, n) for n in range(4)]) for d in (1, 2, 3)
     ]

time: 110 us -> 108 us (0.982)
  waiting for transfers between devices: 18.9 us -> 10.6 us
  blocking collectives: 29.7 us -> 37.5 us
  starting transfers between devices: 50.7 us -> 49.5 us
    ppermute x3, waiting for transfers between devices: 10 us -> 0.78 us  [per_device(): lax.ppermute(gated, 'zh', [((n + d) % 4, n) for n in range(4)])]
    all_gather x4, blocking collectives: 12.5 us -> 20.3 us  [per_device(): both = [lax.all_gather(g, 'core', axis=0, tiled=False) for g in shifted]]
    all_to_all x1, starting transfers between devices: 7.91 us -> 5.98 us  [per_device(): weight = lax.all_to_all(copies_of(own, far), 'y', 0, 0, tiled=True)]
    ppermute x2, starting transfers between devices: 14 us -> 15.5 us  [the longest x1 9.03 us: per_device(): far = lax.ppermute(hold(gated, own), 'zl', [(0, 1), (1, 0)])]
  transfers between devices with their start and end apart: 8 -> 8, of which waited for: 5 -> 4; matrix products, arithmetic and copies ran while one was open for 1% -> 1% of each run, Pallas kernels for 2% -> 2%
where the time goes in v2:
time: 108 us
  starting transfers between devices  49.5 us (46%)
  blocking collectives  37.5 us (35%)
  waiting for transfers between devices  10.6 us (10%)
  Pallas kernels  9.22 us (9%)
    all_gather x4, blocking collectives, per_device(): both = [lax.all_gather(g, 'core', axis=0, tiled=False) for g in shifted]  20.3 us
    all_to_all x1, blocking collectives, per_device(): return finish(lax.all_to_all(parts, 'x', 0, 0, tiled=True))  17.3 us
    ppermute x3, starting transfers between devices, per_device(): lax.ppermute(gated, 'zh', [((n + d) % 4, n) for n in range(4)])  12.4 us
    all_to_all x1, starting transfers between devices, per_device(): got = lax.all_to_all(sent, ('zl', 'y'), 0, 0, tiled=True)  10.7 us
    ppermute x1, starting transfers between devices, per_device(): far = lax.ppermute(hold(gated, own), 'zl', [(0, 1), (1, 0)])  9.03 us
    all_to_all x1, waiting for transfers between devices, per_device(): moved = lax.all_to_all(pack(q, k, v, w.T), 'x', 0, 0, tiled=True)  6.56 us
    ppermute x1, starting transfers between devices, place_weight(): return lax.ppermute(block, ('zl', 'y', 'zh', 'core'), perm)  6.47 us
    all_to_all x1, starting transfers between devices, per_device(): weight = lax.all_to_all(copies_of(own, far), 'y', 0, 0, tiled=True)  5.98 us
  transfers between devices with their start and end apart: 8, of which 4 were waited for; matrix products, arithmetic and copies ran while one was open for 1% of the time, Pallas kernels for 2%

profile of v2, /device:TPU:1, one launch (start us, length us, event | category | flops | bytes accessed | tf_op | source)
XLA Modules:
  0.0 107.9 jit_solution(7682229915041435508)
XLA Ops:
  0.0 0.0 copy-start
  0.0 2.1 %pack.1 = bf16[4,576,128]{2,1,0:T(8,128)(2,1)} custom-call(bf16[512,256]{1,0:T(8,128)(2,1)} %q_hbm.1, bf16[512,256]{1,0:T(8,128)(2,1)} %k_hbm.1, bf16[512,256]{1,0:T(8,128)(2,1)} %v_hbm.1, bf16[64,512]{1,0:T(8,128)(2,1)} %bitcast.19), custom_call_target="tpu_custom_call" | custom-call | tf_op jit(solution)/shard_map/pack/pallas_call | solution.py:39
  2.2 4.9 %all-to-all-start = ((bf16[4,576,128]{2,1,0:T(8,128)(2,1)}), bf16[4,576,128]{2,1,0:T(8,128)(2,1)S(1)}, u32[]{:S(2)}, u32[]{:S(2)}) async-start(bf16[4,576,128]{2,1,0:T(8,128)(2,1)} %pack.1), calls=%async_computation | async-start | bytes 1179648 | tf_op jit(solution)/shard_map/all_to_all | solution.py:239
  7.0 0.7 multiply_bitcast_fusion
  7.7 6.6 %all-to-all-done.moved_ref = bf16[4,576,128]{2,1,0:T(8,128)(2,1)S(1)} async-done(((bf16[4,576,128]{2,1,0:T(8,128)(2,1)}), bf16[4,576,128]{2,1,0:T(8,128)(2,1)S(1)}, u32[]{:S(2)}, u32[]{:S(2)}) %all-to-all-start) | async-done | bytes 589856 | tf_op jit(solution)/shard_map/all_to_all | solution.py:239
  14.3 1.5 %ends.1 = (f32[128,128]{1,0:T(8,128)S(1)}, f32[16,16,128]{2,1,0:T(8,128)}) custom-call(bf16[4,576,128]{2,1,0:T(8,128)(2,1)S(1)} %all-to-all-done.moved_ref, f32[16,128]{1,0:T(8,128)S(1)} %get-tuple-element.10.rate_ref), custom_call_target="tpu_custom_call" | custom-call | tf_op jit(solution)/shard_map/ends/pallas_call | solution.py:79
  15.8 10.7 %all-to-all-start.1 = ((f32[16,16,128]{2,1,0:T(8,128)}), f32[16,16,128]{2,1,0:T(8,128)S(1)}, u32[]{:S(2)}, u32[]{:S(2)}) async-start(f32[16,16,128]{2,1,0:T(8,128)} %get-tuple-element.8), calls=%async_computation.1 | async-start | bytes 262144 | tf_op jit(solution)/shard_map/all_to_all | solution.py:244
  26.6 6.5 %collective-permute-start = (bf16[256,128]{1,0:T(8,128)(2,1)S(1)}, bf16[256,128]{1,0:T(8,128)(2,1)S(1)}, u32[]{:S(2)}, u32[]{:S(2)}) collective-permute-start(bf16[256,128]{1,0:T(8,128)(2,1)S(1)} %bitcast.20), channel_id=1, source_target_pairs={{0,0},{1,64},{2,128},{3,192},{4,256},{5,320},{6,384},{7,448},{32,3... | collective-permute-start | bytes 196616 | tf_op jit(solution)/shard_map/ppermute | solution.py:232
  33.1 0.0 copy-done
  33.1 0.1 dynamic-slice_bitcast_fusion.skip_ref
  33.2 0.9 all-to-all-done.1.got_ref
  34.1 1.8 %scan.1.after_ref = bf16[1024,128]{1,0:T(8,128)(2,1)S(1)} custom-call(s32[1]{0:T(128)} %bitcast.4.me_ref, bf16[4,576,128]{2,1,0:T(8,128)(2,1)S(1)} %all-to-all-done.moved_ref, f32[16,128]{1,0:T(8,128)S(1)} %get-tuple-element.10.rate_ref, f32[16,128]{1,0:T(8,128)S(1)} %get-tuple-element.9.amp_ref, f32[1,128]{1,0:T(1,128)S(1)} %dynamic-slice_bitcast_fusion.skip_ref, ...), custom_call_target="tpu_custom_call" | custom-call | tf_op jit(solution)/shard_map/scan/pallas_call | solution.py:131
  35.9 0.0 collective-permute-done.own_ref
  35.9 9.0 %collective-permute-start.1 = (bf16[256,128]{1,0:T(8,128)(2,1)S(1)}, bf16[256,128]{1,0:T(8,128)(2,1)S(1)}, u32[]{:S(2)}, u32[]{:S(2)}) collective-permute-start(bf16[256,128]{1,0:T(8,128)(2,1)S(1)} %hold.1), channel_id=1, source_target_pairs={{0,256},{256,0},{1,257},{257,1},{2,258},{258,2},{3,259},{259,3},{4... | collective-permute-start | bytes 196616 | tf_op jit(solution)/shard_map/ppermute | solution.py:247
  44.9 2.3 %collective-permute-done.1.far_ref = bf16[256,128]{1,0:T(8,128)(2,1)S(1)} collective-permute-done((bf16[256,128]{1,0:T(8,128)(2,1)S(1)}, bf16[256,128]{1,0:T(8,128)(2,1)S(1)}, u32[]{:S(2)}, u32[]{:S(2)}) %collective-permute-start.1) | collective-permute-done | bytes 65568 | tf_op jit(solution)/shard_map/ppermute | solution.py:247
  47.3 1.1 %copies.1 = bf16[8,2,256,128]{3,2,1,0:T(8,128)(2,1)} custom-call(bf16[256,128]{1,0:T(8,128)(2,1)S(1)} %collective-permute-done.own_ref, bf16[256,128]{1,0:T(8,128)(2,1)S(1)} %collective-permute-done.1.far_ref), custom_call_target="tpu_custom_call" | custom-call | tf_op jit(solution)/shard_map/copies/pallas_call | solution.py:167
  48.4 6.0 %all-to-all-start.2 = ((bf16[8,2,256,128]{3,2,1,0:T(8,128)(2,1)}), bf16[8,2,256,128]{3,2,1,0:T(8,128)(2,1)S(1)}, u32[]{:S(2)}, u32[]{:S(2)}) async-start(bf16[8,2,256,128]{3,2,1,0:T(8,128)(2,1)} %copies.1), calls=%async_computation.2 | async-start | bytes 2097152 | tf_op jit(solution)/shard_map/all_to_all | solution.py:248
  54.3 5.0 %collective-permute-start.3 = (bf16[1024,128]{1,0:T(8,128)(2,1)S(1)}, bf16[1024,128]{1,0:T(8,128)(2,1)S(1)}, u32[]{:S(2)}, u32[]{:S(2)}) collective-permute-start(bf16[1024,128]{1,0:T(8,128)(2,1)S(1)} %scan.1.after_ref), channel_id=1, source_target_pairs={{4,0},{6,2},{0,4},{2,6},{5,1},{7,3},{1,5},{3,7},{12,8},{14,10},{8,... | collective-permute-start | bytes 786440 | tf_op jit(solution)/shard_map/ppermute | solution.py:250
  59.4 0.1 pad_add_fusion.place_ref
  59.5 4.8 %collective-permute-start.4 = (bf16[1024,128]{1,0:T(8,128)(2,1)S(1)}, bf16[1024,128]{1,0:T(8,128)(2,1)S(1)}, u32[]{:S(2)}, u32[]{:S(2)}) collective-permute-start(bf16[1024,128]{1,0:T(8,128)(2,1)S(1)} %scan.1.after_ref), channel_id=1, source_target_pairs={{6,0},{0,2},{2,4},{4,6},{7,1},{1,3},{3,5},{5,7},{14,8},{8,10},{10,... | collective-permute-start | bytes 786440 | tf_op jit(solution)/shard_map/ppermute | solution.py:250
  64.3 2.6 %collective-permute-start.2 = (bf16[1024,128]{1,0:T(8,128)(2,1)S(1)}, bf16[1024,128]{1,0:T(8,128)(2,1)S(1)}, u32[]{:S(2)}, u32[]{:S(2)}) collective-permute-start(bf16[1024,128]{1,0:T(8,128)(2,1)S(1)} %scan.1.after_ref), channel_id=1, source_target_pairs={{2,0},{4,2},{6,4},{0,6},{3,1},{5,3},{7,5},{1,7},{10,8},{12,10},{14... | collective-permute-start | bytes 786440 | tf_op jit(solution)/shard_map/ppermute | solution.py:250
  66.9 8.3 %all-gather = bf16[2048,128]{1,0:T(8,128)(2,1)S(1)} all-gather(bf16[1024,128]{1,0:T(8,128)(2,1)S(1)} %scan.1.after_ref), channel_id=2, replica_groups=mesh['zl'=2,'y'=8,'x'=4,'zh'=4,'core'=2] {'core'}, dimensions={0}, use_global_device_ids=true | all-gather | bytes 786432 | tf_op jit(solution)/shard_map/all_gather | solution.py:252
  75.1 0.0 collective-permute-done.3
  75.1 6.8 %all-gather.2 = bf16[2048,128]{1,0:T(8,128)(2,1)S(1)} all-gather(bf16[1024,128]{1,0:T(8,128)(2,1)S(1)} %collective-permute-done.3), channel_id=4, replica_groups=mesh['zl'=2,'y'=8,'x'=4,'zh'=4,'core'=2] {'core'}, dimensions={0}, use_global_device_ids=true | all-gather | bytes 786432 | tf_op jit(solution)/shard_map/all_gather | solution.py:252
  82.0 0.0 collective-permute-done.4
  82.0 2.9 %all-gather.3 = bf16[2048,128]{1,0:T(8,128)(2,1)S(1)} all-gather(bf16[1024,128]{1,0:T(8,128)(2,1)S(1)} %collective-permute-done.4), channel_id=5, replica_groups=mesh['zl'=2,'y'=8,'x'=4,'zh'=4,'core'=2] {'core'}, dimensions={0}, use_global_device_ids=true | all-gather | bytes 786432 | tf_op jit(solution)/shard_map/all_gather | solution.py:252
  84.9 0.8 collective-permute-done.2
  85.6 2.3 %all-gather.1 = bf16[2048,128]{1,0:T(8,128)(2,1)S(1)} all-gather(bf16[1024,128]{1,0:T(8,128)(2,1)S(1)} %collective-permute-done.2), channel_id=3, replica_groups=mesh['zl'=2,'y'=8,'x'=4,'zh'=4,'core'=2] {'core'}, dimensions={0}, use_global_device_ids=true | all-gather | bytes 786432 | tf_op jit(solution)/shard_map/all_gather | solution.py:252
  87.9 0.0 all-to-all-done.2.w_ref
  87.9 1.8 %project.1 = bf16[4,512,256]{2,1,0:T(8,128)(2,1)S(1)} custom-call(s32[2]{0:T(128)S(1)} %pad_add_fusion.place_ref, bf16[8,2,256,128]{3,2,1,0:T(8,128)(2,1)S(1)} %all-to-all-done.2.w_ref, bf16[2,1024,128]{2,1,0:T(8,128)(2,1)S(1)} %bitcast.15, bf16[2,1024,128]{2,1,0:T(8,128)(2,1)S(1)} %bitcast.18, bf16[2,1024,128]{2,1,0:T(8,128)(2,1)S(1)} %bitcast.16, ...), custom_call_target="tpu_custom_call" | custom-call | tf_op jit(solution)/shard_map/project/pallas_call | solution.py:201
  89.8 17.3 %all_to_all.20.parts_ref = bf16[4,512,256]{2,1,0:T(8,128)(2,1)S(1)} all-to-all(bf16[4,512,256]{2,1,0:T(8,128)(2,1)S(1)} %project.1), channel_id=1, replica_groups=mesh['zl'=2,'y'=8,'x'=4,'zh'=4,'core'=2] {'x'}, dimensions={0} | all-to-all | bytes 2097152 | tf_op jit(solution)/shard_map/all_to_all | solution.py:254
  107.0 0.8 finish.1
  (2 shorter events, 0.0 us)
Async XLA Ops:
  0.0 33.1 %copy-start = (f32[512]{0:T(512)S(1)}, f32[512]{0:T(512)}, u32[]{:S(2)}) copy-start(f32[512]{0:T(512)} %param.13) | copy-start | bytes 6148
  2.2 12.1 %all-to-all-start = ((bf16[4,576,128]{2,1,0:T(8,128)(2,1)}), bf16[4,576,128]{2,1,0:T(8,128)(2,1)S(1)}, u32[]{:S(2)}, u32[]{:S(2)}) async-start(bf16[4,576,128]{2,1,0:T(8,128)(2,1)} %pack.1), calls=%async_computation | async-start | bytes 1179648 | tf_op jit(solution)/shard_map/all_to_all | solution.py:239
  15.8 18.2 %all-to-all-start.1 = ((f32[16,16,128]{2,1,0:T(8,128)}), f32[16,16,128]{2,1,0:T(8,128)S(1)}, u32[]{:S(2)}, u32[]{:S(2)}) async-start(f32[16,16,128]{2,1,0:T(8,128)} %get-tuple-element.8), calls=%async_computation.1 | async-start | bytes 262144 | tf_op jit(solution)/shard_map/all_to_all | solution.py:244
  26.6 9.3 %collective-permute-start = (bf16[256,128]{1,0:T(8,128)(2,1)S(1)}, bf16[256,128]{1,0:T(8,128)(2,1)S(1)}, u32[]{:S(2)}, u32[]{:S(2)}) collective-permute-start(bf16[256,128]{1,0:T(8,128)(2,1)S(1)} %bitcast.20), channel_id=1, source_target_pairs={{0,0},{1,64},{2,128},{3,192},{4,256},{5,320},{6,384},{7,448},{32,3... | collective-permute-start | bytes 196616 | tf_op jit(solution)/shard_map/ppermute | solution.py:232
  35.9 11.4 %collective-permute-start.1 = (bf16[256,128]{1,0:T(8,128)(2,1)S(1)}, bf16[256,128]{1,0:T(8,128)(2,1)S(1)}, u32[]{:S(2)}, u32[]{:S(2)}) collective-permute-start(bf16[256,128]{1,0:T(8,128)(2,1)S(1)} %hold.1), channel_id=1, source_target_pairs={{0,256},{256,0},{1,257},{257,1},{2,258},{258,2},{3,259},{259,3},{4... | collective-permute-start | bytes 196616 | tf_op jit(solution)/shard_map/ppermute | solution.py:247
  48.4 39.6 %all-to-all-start.2 = ((bf16[8,2,256,128]{3,2,1,0:T(8,128)(2,1)}), bf16[8,2,256,128]{3,2,1,0:T(8,128)(2,1)S(1)}, u32[]{:S(2)}, u32[]{:S(2)}) async-start(bf16[8,2,256,128]{3,2,1,0:T(8,128)(2,1)} %copies.1), calls=%async_computation.2 | async-start | bytes 2097152 | tf_op jit(solution)/shard_map/all_to_all | solution.py:248
  54.3 20.8 %collective-permute-start.3 = (bf16[1024,128]{1,0:T(8,128)(2,1)S(1)}, bf16[1024,128]{1,0:T(8,128)(2,1)S(1)}, u32[]{:S(2)}, u32[]{:S(2)}) collective-permute-start(bf16[1024,128]{1,0:T(8,128)(2,1)S(1)} %scan.1.after_ref), channel_id=1, source_target_pairs={{4,0},{6,2},{0,4},{2,6},{5,1},{7,3},{1,5},{3,7},{12,8},{14,10},{8,... | collective-permute-start | bytes 786440 | tf_op jit(solution)/shard_map/ppermute | solution.py:250
  59.5 22.5 %collective-permute-start.4 = (bf16[1024,128]{1,0:T(8,128)(2,1)S(1)}, bf16[1024,128]{1,0:T(8,128)(2,1)S(1)}, u32[]{:S(2)}, u32[]{:S(2)}) collective-permute-start(bf16[1024,128]{1,0:T(8,128)(2,1)S(1)} %scan.1.after_ref), channel_id=1, source_target_pairs={{6,0},{0,2},{2,4},{4,6},{7,1},{1,3},{3,5},{5,7},{14,8},{8,10},{10,... | collective-permute-start | bytes 786440 | tf_op jit(solution)/shard_map/ppermute | solution.py:250
  64.3 21.4 %collective-permute-start.2 = (bf16[1024,128]{1,0:T(8,128)(2,1)S(1)}, bf16[1024,128]{1,0:T(8,128)(2,1)S(1)}, u32[]{:S(2)}, u32[]{:S(2)}) collective-permute-start(bf16[1024,128]{1,0:T(8,128)(2,1)S(1)} %scan.1.after_ref), channel_id=1, source_target_pairs={{2,0},{4,2},{6,4},{0,6},{3,1},{5,3},{7,5},{1,7},{10,8},{12,10},{14... | collective-permute-start | bytes 786440 | tf_op jit(solution)/shard_map/ppermute | solution.py:250

commit v3 on v2

--- a/solution.py
+++ b/solution.py
@@ -17,8 +17,8 @@
 BF16 = jnp.bfloat16
 
 
-def pack_kernel(q_hbm, k_hbm, v_hbm, w_hbm, out_ref, q_ref, k_ref, v_ref, w_ref, sems):
-    pairs = ((k_hbm, k_ref), (v_hbm, v_ref), (q_hbm, q_ref), (w_hbm, w_ref))
+def pack_kernel(q_hbm, k_hbm, v_hbm, out_ref, q_ref, k_ref, v_ref, sems):
+    pairs = ((k_hbm, k_ref), (v_hbm, v_ref), (q_hbm, q_ref))
     copies = [pltpu.make_async_copy(*pair, sems.at[n]) for n, pair in enumerate(pairs)]
     for copy in copies:
         copy.start()
@@ -30,22 +30,18 @@
     copies[2].wait()
     for j in range(4):
         out_ref[j, BLOCK : 2 * BLOCK, :] = q_ref[WIDE * j : WIDE * (j + 1), :].T
-    copies[3].wait()
-    for j in range(4):
-        out_ref[j, 2 * BLOCK :, :] = w_ref[:, WIDE * j : WIDE * (j + 1)]
-
-
-def pack(q, k, v, w):
+
+
+def pack(q, k, v):
     return pl.pallas_call(
         pack_kernel,
-        in_specs=[pl.BlockSpec(memory_space=pltpu.HBM)] * 4,
+        in_specs=[pl.BlockSpec(memory_space=pltpu.HBM)] * 3,
         out_specs=pl.BlockSpec(memory_space=pltpu.VMEM),
-        out_shape=jax.ShapeDtypeStruct((4, 2 * BLOCK + 64, WIDE), BF16),
-        scratch_shapes=[pltpu.VMEM((4 * WIDE, BLOCK), BF16)] * 3
-        + [pltpu.VMEM((64, 4 * WIDE), BF16), pltpu.SemaphoreType.DMA((4,))],
+        out_shape=jax.ShapeDtypeStruct((4, 2 * BLOCK, WIDE), BF16),
+        scratch_shapes=[pltpu.VMEM((4 * WIDE, BLOCK), BF16)] * 3 + [pltpu.SemaphoreType.DMA((3,))],
         compiler_params=pltpu.CompilerParams(vmem_limit_bytes=60 * 1024 * 1024),
         name="pack",
-    )(q, k, v, w)
+    )(q, k, v)
 
 
 def load_product(moved_ref, p_ref):
@@ -53,7 +49,8 @@
         p_ref[BLOCK * j : BLOCK * (j + 1), :] = moved_ref[j, 0:BLOCK, :].astype(F32)
 
 
-def ends_kernel(moved_ref, rate_ref, ends_ref, sent_ref, p_ref):
+def ends_kernel(moved_ref, rate_ref, after_ref, ends_ref, sent_ref, p_ref):
+    del after_ref
     load_product(moved_ref, p_ref)
     rate = rate_ref[...]
     ratio = jnp.exp(-rate)
@@ -75,9 +72,11 @@
         sent_ref[g] = total
 
 
-def ends_call(moved, rate):
+def ends_call(moved, rate, after):
+    vmem = pl.BlockSpec(memory_space=pltpu.VMEM)
     return pl.pallas_call(
         ends_kernel,
+        in_specs=[vmem, vmem, pl.BlockSpec(memory_space=pl.ANY)],
         out_shape=[
             jax.ShapeDtypeStruct((CHUNKS * MODES, WIDE), F32),
             jax.ShapeDtypeStruct((16, MODES, WIDE), F32),
@@ -85,7 +84,7 @@
         scratch_shapes=[pltpu.VMEM((SPAN, WIDE), F32)],
         compiler_params=VMEM,
         name="ends",
-    )(moved, rate)
+    )(moved, rate, after)
 
 
 def scan_kernel(me_ref, moved_ref, rate_ref, amp_ref, skip_ref, ends_ref, got_ref, out_ref, p_ref, y_ref, first_ref):
@@ -142,31 +141,18 @@
     )(me, moved, rate, amp, skip, ends, got)
 
 
-def hold_kernel(after_ref, own_ref, out_ref):
-    del after_ref
-    out_ref[...] = own_ref[...]
-
-
-def hold(after, own):
-    return pl.pallas_call(
-        hold_kernel,
-        in_specs=[pl.BlockSpec(memory_space=pl.ANY), pl.BlockSpec(memory_space=pltpu.VMEM)],
-        out_shape=jax.ShapeDtypeStruct(own.shape, BF16),
-        compiler_params=VMEM,
-        name="hold",
-    )(after, own)
-
-
 def copies_kernel(own_ref, far_ref, out_ref):
-    for n in range(8):
-        out_ref[n, 0] = own_ref[...]
-        out_ref[n, 1] = far_ref[...]
+    for side, ref in enumerate((own_ref, far_ref)):
+        for j in range(4):
+            piece = ref[:, WIDE * j : WIDE * (j + 1)]
+            for y in range(8):
+                out_ref[4 * y + j, side] = piece
 
 
 def copies_of(own, far):
     return pl.pallas_call(
         copies_kernel,
-        out_shape=jax.ShapeDtypeStruct((8, 2, 256, WIDE), BF16),
+        out_shape=jax.ShapeDtypeStruct((32, 2, 64, WIDE), BF16),
         compiler_params=VMEM,
         name="copies",
     )(own, far)
@@ -184,7 +170,8 @@
                 weights, values = [], []
                 for core in range(2):
                     t = 2 * owner + core
-                    weights.append(w_ref[2 * lax.rem(t, 4) + h, lax.rem(t // 4 + zl, 2)])
+                    place, side = 2 * lax.rem(t, 4) + h, lax.rem(t // 4 + zl, 2)
+                    weights.append(jnp.concatenate([w_ref[4 * place + n, side] for n in range(4)], axis=0))
                     values.append(g_ref[core, tokens, :])
                 total += lax.dot_general(
                     jnp.concatenate(weights, axis=1),
@@ -236,16 +223,16 @@
     x = lax.axis_index("x")
     zh, zl = lax.axis_index("zh"), lax.axis_index("zl")
     me = (zl * 8 + lax.axis_index("y")).reshape(1)
-    moved = lax.all_to_all(pack(q, k, v, w.T), "x", 0, 0, tiled=True)
+    own = place_weight(w.T)
+    moved = lax.all_to_all(pack(q, k, v), "x", 0, 0, tiled=True)
     rate = lax.dynamic_slice_in_dim(decay, x * WIDE, WIDE, 0).T / TOTAL
     amp = lax.dynamic_slice_in_dim(residue, x * WIDE, WIDE, 0).T * jnp.sqrt(2.0 * rate)
     own_skip = lax.dynamic_slice_in_dim(skip, x * WIDE, WIDE, 0)[None]
-    ends, sent = ends_call(moved, rate)
+    ends, sent = ends_call(moved, rate, own)
     got = lax.all_to_all(sent, ("zl", "y"), 0, 0, tiled=True)
-    own = place_weight(moved[:, 2 * BLOCK :, :].reshape(256, WIDE))
+    far = lax.ppermute(own, "zl", [(0, 1), (1, 0)])
+    weight = lax.all_to_all(copies_of(own, far), ("y", "x"), 0, 0, tiled=True)
     gated = scan_call(me, moved, rate, amp, own_skip, ends, got)
-    far = lax.ppermute(hold(gated, own), "zl", [(0, 1), (1, 0)])
-    weight = lax.all_to_all(copies_of(own, far), "y", 0, 0, tiled=True)
     shifted = [gated] + [
         lax.ppermute(gated, "zh", [((n + d) % 4, n) for n in range(4)]) for d in (1, 2, 3)
     ]

time: 108 us -> 106 us (0.981)
  waiting for transfers between devices: 10.6 us -> 4.35 us
  blocking collectives: 37.5 us -> 41.5 us
    all_to_all x2, waiting for transfers between devices: 6.57 us -> 0.01 us  [the longest x1 0.01 us: per_device(): moved = lax.all_to_all(pack(q, k, v), 'x', 0, 0, tiled=True)]
    ppermute x1, starting transfers between devices: 9.03 us -> 3.27 us  [per_device(): far = lax.ppermute(own, 'zl', [(0, 1), (1, 0)])]
    all_to_all x1, starting transfers between devices: 10.7 us -> 15 us  [per_device(): got = lax.all_to_all(sent, ('zl', 'y'), 0, 0, tiled=True)]
    all_to_all x2, starting transfers between devices: 10.8 us -> 14.1 us  [the longest x1 9.14 us: per_device(): weight = lax.all_to_all(copies_of(own, far), ('y', 'x'), 0, 0, tiled=True)]
    all_gather x4, blocking collectives: 20.3 us -> 23.5 us  [per_device(): both = [lax.all_gather(g, 'core', axis=0, tiled=False) for g in shifted]]
    ppermute x1, starting transfers between devices: 6.47 us -> 5.05 us  [place_weight(): return lax.ppermute(block, ('zl', 'y', 'zh', 'core'), perm)]
    ppermute x1, waiting for transfers between devices: 0.01 us -> 1.2 us  [place_weight(): return lax.ppermute(block, ('zl', 'y', 'zh', 'core'), perm)]
    pallas_call x3 -> x2, Pallas kernels: 2.66 us -> 2.67 us  [the longest x1 1.55 us: ends_call(): pl.pallas_call(ends_kernel, in_specs=[vmem, vmem, pl.BlockSpec(memory_spa...]
  transfers between devices with their start and end apart: 8 -> 8, of which waited for: 4 -> 3; matrix products, arithmetic and copies ran while one was open for 1% -> 1% of each run, Pallas kernels for 2% -> 3%
where the time goes in v3:
time: 106 us
  starting transfers between devices  49.6 us (47%)
  blocking collectives  41.5 us (39%)
  Pallas kernels  9.18 us (9%)
  waiting for transfers between devices  4.35 us (4%)
    all_gather x4, blocking collectives, per_device(): both = [lax.all_gather(g, 'core', axis=0, tiled=False) for g in shifted]  23.5 us
    all_to_all x1, blocking collectives, per_device(): return finish(lax.all_to_all(parts, 'x', 0, 0, tiled=True))  18 us
    all_to_all x1, starting transfers between devices, per_device(): got = lax.all_to_all(sent, ('zl', 'y'), 0, 0, tiled=True)  15 us
    ppermute x3, starting transfers between devices, per_device(): lax.ppermute(gated, 'zh', [((n + d) % 4, n) for n in range(4)])  12.1 us
    all_to_all x1, starting transfers between devices, per_device(): weight = lax.all_to_all(copies_of(own, far), ('y', 'x'), 0, 0, tiled=True)  9.14 us
    ppermute x1, starting transfers between devices, place_weight(): return lax.ppermute(block, ('zl', 'y', 'zh', 'core'), perm)  5.05 us
    all_to_all x1, starting transfers between devices, per_device(): moved = lax.all_to_all(pack(q, k, v), 'x', 0, 0, tiled=True)  4.99 us
    ppermute x1, starting transfers between devices, per_device(): far = lax.ppermute(own, 'zl', [(0, 1), (1, 0)])  3.27 us
  transfers between devices with their start and end apart: 8, of which 3 were waited for; matrix products, arithmetic and copies ran while one was open for 1% of the time, Pallas kernels for 3%

profile of v3, /device:TPU:1, one launch (start us, length us, event | category | flops | bytes accessed | tf_op | source)
XLA Modules:
  0.0 105.6 jit_solution(10502809208187985619)
XLA Ops:
  0.0 0.0 copy-start
  0.0 2.1 %pack.1 = bf16[4,512,128]{2,1,0:T(8,128)(2,1)} custom-call(bf16[512,256]{1,0:T(8,128)(2,1)} %q_hbm.1, bf16[512,256]{1,0:T(8,128)(2,1)} %k_hbm.1, bf16[512,256]{1,0:T(8,128)(2,1)} %v_hbm.1), custom_call_target="tpu_custom_call" | custom-call | tf_op jit(solution)/shard_map/pack/pallas_call | solution.py:36
  2.1 0.0 copy-start.1
  2.1 5.0 %all-to-all-start.1 = ((bf16[4,512,128]{2,1,0:T(8,128)(2,1)}), bf16[4,512,128]{2,1,0:T(8,128)(2,1)S(1)}, u32[]{:S(2)}, u32[]{:S(2)}) async-start(bf16[4,512,128]{2,1,0:T(8,128)(2,1)} %pack.1), calls=%async_computation.1 | async-start | bytes 1048576 | tf_op jit(solution)/shard_map/all_to_all | solution.py:227
  7.1 0.0 copy-done.1
  7.1 5.0 %collective-permute-start = (bf16[64,512]{1,0:T(8,128)(2,1)S(1)}, bf16[64,512]{1,0:T(8,128)(2,1)S(1)}, u32[]{:S(2)}, u32[]{:S(2)}) collective-permute-start(bf16[64,512]{1,0:T(8,128)(2,1)S(1)} %bitcast.18), channel_id=1, source_target_pairs={{0,0},{1,64},{2,128},{3,192},{4,256},{5,320},{6,384},{7,448},{32,3... | collective-permute-start | bytes 196616 | tf_op jit(solution)/shard_map/ppermute | solution.py:219
  12.2 0.7 multiply_bitcast_fusion
  12.9 1.2 %collective-permute-done.own_ref.after_ref = bf16[64,512]{1,0:T(8,128)(2,1)S(1)} collective-permute-done((bf16[64,512]{1,0:T(8,128)(2,1)S(1)}, bf16[64,512]{1,0:T(8,128)(2,1)S(1)}, u32[]{:S(2)}, u32[]{:S(2)}) %collective-permute-start) | collective-permute-done | bytes 65568 | tf_op jit(solution)/shard_map/ppermute | solution.py:219
  14.1 0.0 all-to-all-done.1.moved_ref
  14.1 1.5 %ends.1 = (f32[128,128]{1,0:T(8,128)S(1)}, f32[16,16,128]{2,1,0:T(8,128)}) custom-call(bf16[4,512,128]{2,1,0:T(8,128)(2,1)S(1)} %all-to-all-done.1.moved_ref, f32[16,128]{1,0:T(8,128)S(1)} %get-tuple-element.10.rate_ref, bf16[64,512]{1,0:T(8,128)(2,1)S(1)} %collective-permute-done.own_ref.after_ref), custom_call_target="tpu_custom_call" | custom-call | tf_op jit(solution)/shard_map/ends/pallas_call | solution.py:77
  15.7 15.0 %all-to-all-start.2 = ((f32[16,16,128]{2,1,0:T(8,128)}), f32[16,16,128]{2,1,0:T(8,128)S(1)}, u32[]{:S(2)}, u32[]{:S(2)}) async-start(f32[16,16,128]{2,1,0:T(8,128)} %get-tuple-element.8), calls=%async_computation.2 | async-start | bytes 262144 | tf_op jit(solution)/shard_map/all_to_all | solution.py:232
  30.7 3.3 %collective-permute-start.1 = (bf16[64,512]{1,0:T(8,128)(2,1)S(1)}, bf16[64,512]{1,0:T(8,128)(2,1)S(1)}, u32[]{:S(2)}, u32[]{:S(2)}) collective-permute-start(bf16[64,512]{1,0:T(8,128)(2,1)S(1)} %collective-permute-done.own_ref.after_ref), channel_id=1, source_target_pairs={{0,256},{256,0},{1,257},{257,1},{2,258},{258,2},{3,259},{259,3},{4... | collective-permute-start | bytes 196616 | tf_op jit(solution)/shard_map/ppermute | solution.py:233
  34.0 2.0 %collective-permute-done.1.far_ref = bf16[64,512]{1,0:T(8,128)(2,1)S(1)} collective-permute-done((bf16[64,512]{1,0:T(8,128)(2,1)S(1)}, bf16[64,512]{1,0:T(8,128)(2,1)S(1)}, u32[]{:S(2)}, u32[]{:S(2)}) %collective-permute-start.1) | collective-permute-done | bytes 65568 | tf_op jit(solution)/shard_map/ppermute | solution.py:233
  36.0 1.1 %copies.1 = bf16[32,2,64,128]{3,2,1,0:T(8,128)(2,1)} custom-call(bf16[64,512]{1,0:T(8,128)(2,1)S(1)} %collective-permute-done.own_ref.after_ref, bf16[64,512]{1,0:T(8,128)(2,1)S(1)} %collective-permute-done.1.far_ref), custom_call_target="tpu_custom_call" | custom-call | tf_op jit(solution)/shard_map/copies/pallas_call | solution.py:153
  37.1 1.1 %all-to-all-done.2.got_ref = f32[16,16,128]{2,1,0:T(8,128)S(1)} async-done(((f32[16,16,128]{2,1,0:T(8,128)}), f32[16,16,128]{2,1,0:T(8,128)S(1)}, u32[]{:S(2)}, u32[]{:S(2)}) %all-to-all-start.2) | async-done | bytes 131104 | tf_op jit(solution)/shard_map/all_to_all | solution.py:232
  38.2 9.1 %all-to-all-start = ((bf16[32,2,64,128]{3,2,1,0:T(8,128)(2,1)}), bf16[32,2,64,128]{3,2,1,0:T(8,128)(2,1)S(1)}, u32[]{:S(2)}, u32[]{:S(2)}) async-start(bf16[32,2,64,128]{3,2,1,0:T(8,128)(2,1)} %copies.1), calls=%async_computation | async-start | bytes 2097152 | tf_op jit(solution)/shard_map/all_to_all | solution.py:234
  47.4 0.0 copy-done
  47.4 0.1 dynamic-slice_bitcast_fusion.skip_ref
  47.5 1.8 %scan.1 = bf16[1024,128]{1,0:T(8,128)(2,1)S(1)} custom-call(s32[1]{0:T(128)} %bitcast.3.me_ref, bf16[4,512,128]{2,1,0:T(8,128)(2,1)S(1)} %all-to-all-done.1.moved_ref, f32[16,128]{1,0:T(8,128)S(1)} %get-tuple-element.10.rate_ref, f32[16,128]{1,0:T(8,128)S(1)} %get-tuple-element.9.amp_ref, f32[1,128]{1,0:T(1,128)S(1)} %dynamic-slice_bitcast_fusion.skip_ref, ...), custom_call_target="tpu_custom_call" | custom-call | tf_op jit(solution)/shard_map/scan/pallas_call | solution.py:130
  49.2 6.2 %collective-permute-start.2 = (bf16[1024,128]{1,0:T(8,128)(2,1)S(1)}, bf16[1024,128]{1,0:T(8,128)(2,1)S(1)}, u32[]{:S(2)}, u32[]{:S(2)}) collective-permute-start(bf16[1024,128]{1,0:T(8,128)(2,1)S(1)} %scan.1), channel_id=1, source_target_pairs={{2,0},{4,2},{6,4},{0,6},{3,1},{5,3},{7,5},{1,7},{10,8},{12,10},{14... | collective-permute-start | bytes 786440 | tf_op jit(solution)/shard_map/ppermute | solution.py:237
  55.4 0.1 pad_add_fusion.place_ref
  55.5 2.0 %collective-permute-start.3 = (bf16[1024,128]{1,0:T(8,128)(2,1)S(1)}, bf16[1024,128]{1,0:T(8,128)(2,1)S(1)}, u32[]{:S(2)}, u32[]{:S(2)}) collective-permute-start(bf16[1024,128]{1,0:T(8,128)(2,1)S(1)} %scan.1), channel_id=1, source_target_pairs={{4,0},{6,2},{0,4},{2,6},{5,1},{7,3},{1,5},{3,7},{12,8},{14,10},{8,... | collective-permute-start | bytes 786440 | tf_op jit(solution)/shard_map/ppermute | solution.py:237
  57.5 3.9 %collective-permute-start.4 = (bf16[1024,128]{1,0:T(8,128)(2,1)S(1)}, bf16[1024,128]{1,0:T(8,128)(2,1)S(1)}, u32[]{:S(2)}, u32[]{:S(2)}) collective-permute-start(bf16[1024,128]{1,0:T(8,128)(2,1)S(1)} %scan.1), channel_id=1, source_target_pairs={{6,0},{0,2},{2,4},{4,6},{7,1},{1,3},{3,5},{5,7},{14,8},{8,10},{10,... | collective-permute-start | bytes 786440 | tf_op jit(solution)/shard_map/ppermute | solution.py:237
  61.4 7.3 %all-gather = bf16[2048,128]{1,0:T(8,128)(2,1)S(1)} all-gather(bf16[1024,128]{1,0:T(8,128)(2,1)S(1)} %scan.1), channel_id=2, replica_groups=mesh['zl'=2,'y'=8,'x'=4,'zh'=4,'core'=2] {'core'}, dimensions={0}, use_global_device_ids=true | all-gather | bytes 786432 | tf_op jit(solution)/shard_map/all_gather | solution.py:239
  68.8 0.0 collective-permute-done.2
  68.8 11.8 %all-gather.1 = bf16[2048,128]{1,0:T(8,128)(2,1)S(1)} all-gather(bf16[1024,128]{1,0:T(8,128)(2,1)S(1)} %collective-permute-done.2), channel_id=3, replica_groups=mesh['zl'=2,'y'=8,'x'=4,'zh'=4,'core'=2] {'core'}, dimensions={0}, use_global_device_ids=true | all-gather | bytes 786432 | tf_op jit(solution)/shard_map/all_gather | solution.py:239
  80.6 0.0 collective-permute-done.3
  80.6 2.2 %all-gather.2 = bf16[2048,128]{1,0:T(8,128)(2,1)S(1)} all-gather(bf16[1024,128]{1,0:T(8,128)(2,1)S(1)} %collective-permute-done.3), channel_id=4, replica_groups=mesh['zl'=2,'y'=8,'x'=4,'zh'=4,'core'=2] {'core'}, dimensions={0}, use_global_device_ids=true | all-gather | bytes 786432 | tf_op jit(solution)/shard_map/all_gather | solution.py:239
  82.8 0.0 collective-permute-done.4
  82.8 2.2 %all-gather.3 = bf16[2048,128]{1,0:T(8,128)(2,1)S(1)} all-gather(bf16[1024,128]{1,0:T(8,128)(2,1)S(1)} %collective-permute-done.4), channel_id=5, replica_groups=mesh['zl'=2,'y'=8,'x'=4,'zh'=4,'core'=2] {'core'}, dimensions={0}, use_global_device_ids=true | all-gather | bytes 786432 | tf_op jit(solution)/shard_map/all_gather | solution.py:239
  84.9 0.0 all-to-all-done.w_ref
  84.9 1.8 %project.1 = bf16[4,512,256]{2,1,0:T(8,128)(2,1)S(1)} custom-call(s32[2]{0:T(128)S(1)} %pad_add_fusion.place_ref, bf16[32,2,64,128]{3,2,1,0:T(8,128)(2,1)S(1)} %all-to-all-done.w_ref, bf16[2,1024,128]{2,1,0:T(8,128)(2,1)S(1)} %bitcast.14, bf16[2,1024,128]{2,1,0:T(8,128)(2,1)S(1)} %bitcast.15, bf16[2,1024,128]{2,1,0:T(8,128)(2,1)S(1)} %bitcast.16, ...), custom_call_target="tpu_custom_call" | custom-call | tf_op jit(solution)/shard_map/project/pallas_call | solution.py:188
  86.8 18.0 %all_to_all.20.parts_ref = bf16[4,512,256]{2,1,0:T(8,128)(2,1)S(1)} all-to-all(bf16[4,512,256]{2,1,0:T(8,128)(2,1)S(1)} %project.1), channel_id=1, replica_groups=mesh['zl'=2,'y'=8,'x'=4,'zh'=4,'core'=2] {'x'}, dimensions={0} | all-to-all | bytes 2097152 | tf_op jit(solution)/shard_map/all_to_all | solution.py:241
  104.8 0.8 finish.1
Async XLA Ops:
  0.0 47.4 %copy-start = (f32[512]{0:T(512)S(1)}, f32[512]{0:T(512)}, u32[]{:S(2)}) copy-start(f32[512]{0:T(512)} %param.13) | copy-start | bytes 6148
  2.1 5.0 %copy-start.1 = (bf16[512,64]{0,1:T(8,128)(2,1)S(1)}, bf16[512,64]{0,1:T(8,128)(2,1)}, u32[]{:S(2)}) copy-start(bf16[512,64]{0,1:T(8,128)(2,1)} %param.10) | copy-start | bytes 196612
  2.1 12.0 %all-to-all-start.1 = ((bf16[4,512,128]{2,1,0:T(8,128)(2,1)}), bf16[4,512,128]{2,1,0:T(8,128)(2,1)S(1)}, u32[]{:S(2)}, u32[]{:S(2)}) async-start(bf16[4,512,128]{2,1,0:T(8,128)(2,1)} %pack.1), calls=%async_computation.1 | async-start | bytes 1048576 | tf_op jit(solution)/shard_map/all_to_all | solution.py:227
  7.1 7.0 %collective-permute-start = (bf16[64,512]{1,0:T(8,128)(2,1)S(1)}, bf16[64,512]{1,0:T(8,128)(2,1)S(1)}, u32[]{:S(2)}, u32[]{:S(2)}) collective-permute-start(bf16[64,512]{1,0:T(8,128)(2,1)S(1)} %bitcast.18), channel_id=1, source_target_pairs={{0,0},{1,64},{2,128},{3,192},{4,256},{5,320},{6,384},{7,448},{32,3... | collective-permute-start | bytes 196616 | tf_op jit(solution)/shard_map/ppermute | solution.py:219
  15.7 22.6 %all-to-all-start.2 = ((f32[16,16,128]{2,1,0:T(8,128)}), f32[16,16,128]{2,1,0:T(8,128)S(1)}, u32[]{:S(2)}, u32[]{:S(2)}) async-start(f32[16,16,128]{2,1,0:T(8,128)} %get-tuple-element.8), calls=%async_computation.2 | async-start | bytes 262144 | tf_op jit(solution)/shard_map/all_to_all | solution.py:232
  30.7 5.3 %collective-permute-start.1 = (bf16[64,512]{1,0:T(8,128)(2,1)S(1)}, bf16[64,512]{1,0:T(8,128)(2,1)S(1)}, u32[]{:S(2)}, u32[]{:S(2)}) collective-permute-start(bf16[64,512]{1,0:T(8,128)(2,1)S(1)} %collective-permute-done.own_ref.after_ref), channel_id=1, source_target_pairs={{0,256},{256,0},{1,257},{257,1},{2,258},{258,2},{3,259},{259,3},{4... | collective-permute-start | bytes 196616 | tf_op jit(solution)/shard_map/ppermute | solution.py:233
  38.2 46.7 %all-to-all-start = ((bf16[32,2,64,128]{3,2,1,0:T(8,128)(2,1)}), bf16[32,2,64,128]{3,2,1,0:T(8,128)(2,1)S(1)}, u32[]{:S(2)}, u32[]{:S(2)}) async-start(bf16[32,2,64,128]{3,2,1,0:T(8,128)(2,1)} %copies.1), calls=%async_computation | async-start | bytes 2097152 | tf_op jit(solution)/shard_map/all_to_all | solution.py:234
  49.2 19.5 %collective-permute-start.2 = (bf16[1024,128]{1,0:T(8,128)(2,1)S(1)}, bf16[1024,128]{1,0:T(8,128)(2,1)S(1)}, u32[]{:S(2)}, u32[]{:S(2)}) collective-permute-start(bf16[1024,128]{1,0:T(8,128)(2,1)S(1)} %scan.1), channel_id=1, source_target_pairs={{2,0},{4,2},{6,4},{0,6},{3,1},{5,3},{7,5},{1,7},{10,8},{12,10},{14... | collective-permute-start | bytes 786440 | tf_op jit(solution)/shard_map/ppermute | solution.py:237
  55.5 25.1 %collective-permute-start.3 = (bf16[1024,128]{1,0:T(8,128)(2,1)S(1)}, bf16[1024,128]{1,0:T(8,128)(2,1)S(1)}, u32[]{:S(2)}, u32[]{:S(2)}) collective-permute-start(bf16[1024,128]{1,0:T(8,128)(2,1)S(1)} %scan.1), channel_id=1, source_target_pairs={{4,0},{6,2},{0,4},{2,6},{5,1},{7,3},{1,5},{3,7},{12,8},{14,10},{8,... | collective-permute-start | bytes 786440 | tf_op jit(solution)/shard_map/ppermute | solution.py:237
  57.5 25.2 %collective-permute-start.4 = (bf16[1024,128]{1,0:T(8,128)(2,1)S(1)}, bf16[1024,128]{1,0:T(8,128)(2,1)S(1)}, u32[]{:S(2)}, u32[]{:S(2)}) collective-permute-start(bf16[1024,128]{1,0:T(8,128)(2,1)S(1)} %scan.1), channel_id=1, source_target_pairs={{6,0},{0,2},{2,4},{4,6},{7,1},{1,3},{3,5},{5,7},{14,8},{8,10},{10,... | collective-permute-start | bytes 786440 | tf_op jit(solution)/shard_map/ppermute | solution.py:237

commit v4 on v3

--- a/solution.py
+++ b/solution.py
@@ -17,28 +17,34 @@
 BF16 = jnp.bfloat16
 
 
-def pack_kernel(q_hbm, k_hbm, v_hbm, out_ref, q_ref, k_ref, v_ref, sems):
+def pack_kernel(q_hbm, k_hbm, v_hbm, out_hbm, q_ref, k_ref, v_ref, moved_ref, sems, out_sems):
     pairs = ((k_hbm, k_ref), (v_hbm, v_ref), (q_hbm, q_ref))
     copies = [pltpu.make_async_copy(*pair, sems.at[n]) for n, pair in enumerate(pairs)]
     for copy in copies:
         copy.start()
     copies[0].wait()
     copies[1].wait()
-    for j in range(4):
-        rows = slice(WIDE * j, WIDE * (j + 1))
-        out_ref[j, 0:BLOCK, :] = (k_ref[rows, :] * v_ref[rows, :]).T
-    copies[2].wait()
-    for j in range(4):
-        out_ref[j, BLOCK : 2 * BLOCK, :] = q_ref[WIDE * j : WIDE * (j + 1), :].T
+    leaving = []
+    for n in range(8):
+        j, begin = n % 4, BLOCK * (n // 4)
+        if n == 4:
+            copies[2].wait()
+        rows, part = slice(WIDE * j, WIDE * (j + 1)), slice(begin, begin + BLOCK)
+        moved_ref[j, part, :] = (k_ref[rows, :] * v_ref[rows, :] if n < 4 else q_ref[rows, :]).T
+        leaving.append(pltpu.make_async_copy(moved_ref.at[j, part], out_hbm.at[j, part], out_sems.at[n]))
+        leaving[-1].start()
+    for copy in leaving:
+        copy.wait()
 
 
 def pack(q, k, v):
     return pl.pallas_call(
         pack_kernel,
         in_specs=[pl.BlockSpec(memory_space=pltpu.HBM)] * 3,
-        out_specs=pl.BlockSpec(memory_space=pltpu.VMEM),
+        out_specs=pl.BlockSpec(memory_space=pltpu.HBM),
         out_shape=jax.ShapeDtypeStruct((4, 2 * BLOCK, WIDE), BF16),
-        scratch_shapes=[pltpu.VMEM((4 * WIDE, BLOCK), BF16)] * 3 + [pltpu.SemaphoreType.DMA((3,))],
+        scratch_shapes=[pltpu.VMEM((4 * WIDE, BLOCK), BF16)] * 3
+        + [pltpu.VMEM((4, 2 * BLOCK, WIDE), BF16), pltpu.SemaphoreType.DMA((3,)), pltpu.SemaphoreType.DMA((8,))],
         compiler_params=pltpu.CompilerParams(vmem_limit_bytes=60 * 1024 * 1024),
         name="pack",
     )(q, k, v)
@@ -49,8 +55,7 @@
         p_ref[BLOCK * j : BLOCK * (j + 1), :] = moved_ref[j, 0:BLOCK, :].astype(F32)
 
 
-def ends_kernel(moved_ref, rate_ref, after_ref, ends_ref, sent_ref, p_ref):
-    del after_ref
+def ends_kernel(moved_ref, rate_ref, ends_ref, total_ref, p_ref):
     load_product(moved_ref, p_ref)
     rate = rate_ref[...]
     ratio = jnp.exp(-rate)
@@ -68,23 +73,36 @@
     total = ends_ref[0:MODES, :]
     for s in range(1, CHUNKS):
         total = total * over_chunk + ends_ref[MODES * s : MODES * (s + 1), :]
-    for g in range(16):
-        sent_ref[g] = total
-
-
-def ends_call(moved, rate, after):
-    vmem = pl.BlockSpec(memory_space=pltpu.VMEM)
+    total_ref[...] = total
+
+
+def ends_call(moved, rate):
     return pl.pallas_call(
         ends_kernel,
-        in_specs=[vmem, vmem, pl.BlockSpec(memory_space=pl.ANY)],
         out_shape=[
             jax.ShapeDtypeStruct((CHUNKS * MODES, WIDE), F32),
-            jax.ShapeDtypeStruct((16, MODES, WIDE), F32),
+            jax.ShapeDtypeStruct((MODES, WIDE), F32),
         ],
         scratch_shapes=[pltpu.VMEM((SPAN, WIDE), F32)],
         compiler_params=VMEM,
         name="ends",
-    )(moved, rate, after)
+    )(moved, rate)
+
+
+def sent_kernel(total_ref, after_ref, out_ref):
+    del after_ref
+    for g in range(16):
+        out_ref[g] = total_ref[...]
+
+
+def sent_call(total, after):
+    return pl.pallas_call(
+        sent_kernel,
+        in_specs=[pl.BlockSpec(memory_space=pltpu.VMEM), pl.BlockSpec(memory_space=pl.ANY)],
+        out_shape=jax.ShapeDtypeStruct((16, MODES, WIDE), F32),
+        compiler_params=VMEM,
+        name="sent",
+    )(total, after)
 
 
 def scan_kernel(me_ref, moved_ref, rate_ref, amp_ref, skip_ref, ends_ref, got_ref, out_ref, p_ref, y_ref, first_ref):
@@ -228,8 +246,8 @@
     rate = lax.dynamic_slice_in_dim(decay, x * WIDE, WIDE, 0).T / TOTAL
     amp = lax.dynamic_slice_in_dim(residue, x * WIDE, WIDE, 0).T * jnp.sqrt(2.0 * rate)
     own_skip = lax.dynamic_slice_in_dim(skip, x * WIDE, WIDE, 0)[None]
-    ends, sent = ends_call(moved, rate, own)
-    got = lax.all_to_all(sent, ("zl", "y"), 0, 0, tiled=True)
+    ends, total = ends_call(moved, rate)
+    got = lax.all_to_all(sent_call(total, own), ("zl", "y"), 0, 0, tiled=True)
     far = lax.ppermute(own, "zl", [(0, 1), (1, 0)])
     weight = lax.all_to_all(copies_of(own, far), ("y", "x"), 0, 0, tiled=True)
     gated = scan_call(me, moved, rate, amp, own_skip, ends, got)

time: 106 us -> 106 us (level)
    ppermute x1, waiting for transfers between devices: 1.2 us -> 0.01 us  [place_weight(): return lax.ppermute(block, ('zl', 'y', 'zh', 'core'), perm)]
    all_to_all x1, waiting for transfers between devices: 0.01 us -> 1.14 us  [per_device(): moved = lax.all_to_all(pack(q, k, v), 'x', 0, 0, tiled=True)]
  transfers between devices with their start and end apart: 8 -> 8, of which waited for: 3 -> 3; matrix products, arithmetic and copies ran while one was open for 1% -> 1% of each run, Pallas kernels for 3% -> 4%
where the time goes in v4:
time: 106 us; the launch traced here: 105 us
  starting transfers between devices  48.7 us (46%)
  blocking collectives  41.5 us (39%)
  Pallas kernels  9.08 us (9%)
  waiting for transfers between devices  4.29 us (4%)
    all_gather x4, blocking collectives, per_device(): both = [lax.all_gather(g, 'core', axis=0, tiled=False) for g in shifted]  23.5 us
    all_to_all x1, blocking collectives, per_device(): return finish(lax.all_to_all(parts, 'x', 0, 0, tiled=True))  18 us
    all_to_all x1, starting transfers between devices, per_device(): got = lax.all_to_all(sent_call(total, own), ('zl', 'y'), 0, 0, tiled=True)  14.2 us
    ppermute x3, starting transfers between devices, per_device(): lax.ppermute(gated, 'zh', [((n + d) % 4, n) for n in range(4)])  12.1 us
    all_to_all x1, starting transfers between devices, per_device(): weight = lax.all_to_all(copies_of(own, far), ('y', 'x'), 0, 0, tiled=True)  9.14 us
    ppermute x1, starting transfers between devices, place_weight(): return lax.ppermute(block, ('zl', 'y', 'zh', 'core'), perm)  5.05 us
    all_to_all x1, starting transfers between devices, per_device(): moved = lax.all_to_all(pack(q, k, v), 'x', 0, 0, tiled=True)  4.99 us
    ppermute x1, starting transfers between devices, per_device(): far = lax.ppermute(own, 'zl', [(0, 1), (1, 0)])  3.27 us
  transfers between devices with their start and end apart: 8, of which 3 were waited for; matrix products, arithmetic and copies ran while one was open for 1% of the time, Pallas kernels for 4%

profile of v4, /device:TPU:1, one launch (start us, length us, event | category | flops | bytes accessed | tf_op | source)
XLA Modules:
  0.0 104.7 jit_solution(8627670857208291476)
XLA Ops:
  0.0 0.0 copy-start
  0.0 2.0 %pack.1 = bf16[4,512,128]{2,1,0:T(8,128)(2,1)} custom-call(bf16[512,256]{1,0:T(8,128)(2,1)} %q_hbm.1, bf16[512,256]{1,0:T(8,128)(2,1)} %k_hbm.1, bf16[512,256]{1,0:T(8,128)(2,1)} %v_hbm.1), custom_call_target="tpu_custom_call" | custom-call | tf_op jit(solution)/shard_map/pack/pallas_call | solution.py:41
  2.0 0.0 copy-start.1
  2.1 5.0 %all-to-all-start.1 = ((bf16[4,512,128]{2,1,0:T(8,128)(2,1)}), bf16[4,512,128]{2,1,0:T(8,128)(2,1)S(1)}, u32[]{:S(2)}, u32[]{:S(2)}) async-start(bf16[4,512,128]{2,1,0:T(8,128)(2,1)} %pack.1), calls=%async_computation.1 | async-start | bytes 1048576 | tf_op jit(solution)/shard_map/all_to_all | solution.py:245
  7.0 0.0 copy-done.1
  7.1 5.0 %collective-permute-start = (bf16[64,512]{1,0:T(8,128)(2,1)S(1)}, bf16[64,512]{1,0:T(8,128)(2,1)S(1)}, u32[]{:S(2)}, u32[]{:S(2)}) collective-permute-start(bf16[64,512]{1,0:T(8,128)(2,1)S(1)} %bitcast.18), channel_id=1, source_target_pairs={{0,0},{1,64},{2,128},{3,192},{4,256},{5,320},{6,384},{7,448},{32,3... | collective-permute-start | bytes 196616 | tf_op jit(solution)/shard_map/ppermute | solution.py:237
  12.1 0.7 multiply_bitcast_fusion
  12.8 1.1 %all-to-all-done.1.moved_ref = bf16[4,512,128]{2,1,0:T(8,128)(2,1)S(1)} async-done(((bf16[4,512,128]{2,1,0:T(8,128)(2,1)}), bf16[4,512,128]{2,1,0:T(8,128)(2,1)S(1)}, u32[]{:S(2)}, u32[]{:S(2)}) %all-to-all-start.1) | async-done | bytes 524320 | tf_op jit(solution)/shard_map/all_to_all | solution.py:245
  14.0 0.9 ends.1
  14.8 0.0 collective-permute-done.own_ref.after_ref
  14.9 0.7 sent.1
  15.5 14.2 %all-to-all-start.2 = ((f32[16,16,128]{2,1,0:T(8,128)}), f32[16,16,128]{2,1,0:T(8,128)S(1)}, u32[]{:S(2)}, u32[]{:S(2)}) async-start(f32[16,16,128]{2,1,0:T(8,128)} %sent.1), calls=%async_computation.2 | async-start | bytes 262144 | tf_op jit(solution)/shard_map/all_to_all | solution.py:250
  29.7 3.3 %collective-permute-start.1 = (bf16[64,512]{1,0:T(8,128)(2,1)S(1)}, bf16[64,512]{1,0:T(8,128)(2,1)S(1)}, u32[]{:S(2)}, u32[]{:S(2)}) collective-permute-start(bf16[64,512]{1,0:T(8,128)(2,1)S(1)} %collective-permute-done.own_ref.after_ref), channel_id=1, source_target_pairs={{0,256},{256,0},{1,257},{257,1},{2,258},{258,2},{3,259},{259,3},{4... | collective-permute-start | bytes 196616 | tf_op jit(solution)/shard_map/ppermute | solution.py:251
  33.0 2.0 %collective-permute-done.1.far_ref = bf16[64,512]{1,0:T(8,128)(2,1)S(1)} collective-permute-done((bf16[64,512]{1,0:T(8,128)(2,1)S(1)}, bf16[64,512]{1,0:T(8,128)(2,1)S(1)}, u32[]{:S(2)}, u32[]{:S(2)}) %collective-permute-start.1) | collective-permute-done | bytes 65568 | tf_op jit(solution)/shard_map/ppermute | solution.py:251
  35.0 1.1 %copies.1 = bf16[32,2,64,128]{3,2,1,0:T(8,128)(2,1)} custom-call(bf16[64,512]{1,0:T(8,128)(2,1)S(1)} %collective-permute-done.own_ref.after_ref, bf16[64,512]{1,0:T(8,128)(2,1)S(1)} %collective-permute-done.1.far_ref), custom_call_target="tpu_custom_call" | custom-call | tf_op jit(solution)/shard_map/copies/pallas_call | solution.py:171
  36.2 1.1 %all-to-all-done.2.got_ref = f32[16,16,128]{2,1,0:T(8,128)S(1)} async-done(((f32[16,16,128]{2,1,0:T(8,128)}), f32[16,16,128]{2,1,0:T(8,128)S(1)}, u32[]{:S(2)}, u32[]{:S(2)}) %all-to-all-start.2) | async-done | bytes 131104 | tf_op jit(solution)/shard_map/all_to_all | solution.py:250
  37.3 9.1 %all-to-all-start = ((bf16[32,2,64,128]{3,2,1,0:T(8,128)(2,1)}), bf16[32,2,64,128]{3,2,1,0:T(8,128)(2,1)S(1)}, u32[]{:S(2)}, u32[]{:S(2)}) async-start(bf16[32,2,64,128]{3,2,1,0:T(8,128)(2,1)} %copies.1), calls=%async_computation | async-start | bytes 2097152 | tf_op jit(solution)/shard_map/all_to_all | solution.py:252
  46.4 0.0 copy-done
  46.4 0.1 dynamic-slice_bitcast_fusion.skip_ref
  46.5 1.8 %scan.1 = bf16[1024,128]{1,0:T(8,128)(2,1)S(1)} custom-call(s32[1]{0:T(128)} %bitcast.3.me_ref, bf16[4,512,128]{2,1,0:T(8,128)(2,1)S(1)} %all-to-all-done.1.moved_ref, f32[16,128]{1,0:T(8,128)S(1)} %get-tuple-element.10.rate_ref, f32[16,128]{1,0:T(8,128)S(1)} %get-tuple-element.9.amp_ref, f32[1,128]{1,0:T(1,128)S(1)} %dynamic-slice_bitcast_fusion.skip_ref, ...), custom_call_target="tpu_custom_call" | custom-call | tf_op jit(solution)/shard_map/scan/pallas_call | solution.py:148
  48.3 6.2 %collective-permute-start.2 = (bf16[1024,128]{1,0:T(8,128)(2,1)S(1)}, bf16[1024,128]{1,0:T(8,128)(2,1)S(1)}, u32[]{:S(2)}, u32[]{:S(2)}) collective-permute-start(bf16[1024,128]{1,0:T(8,128)(2,1)S(1)} %scan.1), channel_id=1, source_target_pairs={{2,0},{4,2},{6,4},{0,6},{3,1},{5,3},{7,5},{1,7},{10,8},{12,10},{14... | collective-permute-start | bytes 786440 | tf_op jit(solution)/shard_map/ppermute | solution.py:255
  54.5 0.1 pad_add_fusion.place_ref
  54.5 2.0 %collective-permute-start.3 = (bf16[1024,128]{1,0:T(8,128)(2,1)S(1)}, bf16[1024,128]{1,0:T(8,128)(2,1)S(1)}, u32[]{:S(2)}, u32[]{:S(2)}) collective-permute-start(bf16[1024,128]{1,0:T(8,128)(2,1)S(1)} %scan.1), channel_id=1, source_target_pairs={{4,0},{6,2},{0,4},{2,6},{5,1},{7,3},{1,5},{3,7},{12,8},{14,10},{8,... | collective-permute-start | bytes 786440 | tf_op jit(solution)/shard_map/ppermute | solution.py:255
  56.6 3.9 %collective-permute-start.4 = (bf16[1024,128]{1,0:T(8,128)(2,1)S(1)}, bf16[1024,128]{1,0:T(8,128)(2,1)S(1)}, u32[]{:S(2)}, u32[]{:S(2)}) collective-permute-start(bf16[1024,128]{1,0:T(8,128)(2,1)S(1)} %scan.1), channel_id=1, source_target_pairs={{6,0},{0,2},{2,4},{4,6},{7,1},{1,3},{3,5},{5,7},{14,8},{8,10},{10,... | collective-permute-start | bytes 786440 | tf_op jit(solution)/shard_map/ppermute | solution.py:255
  60.5 7.3 %all-gather = bf16[2048,128]{1,0:T(8,128)(2,1)S(1)} all-gather(bf16[1024,128]{1,0:T(8,128)(2,1)S(1)} %scan.1), channel_id=2, replica_groups=mesh['zl'=2,'y'=8,'x'=4,'zh'=4,'core'=2] {'core'}, dimensions={0}, use_global_device_ids=true | all-gather | bytes 786432 | tf_op jit(solution)/shard_map/all_gather | solution.py:257
  67.8 0.0 collective-permute-done.2
  67.8 11.8 %all-gather.1 = bf16[2048,128]{1,0:T(8,128)(2,1)S(1)} all-gather(bf16[1024,128]{1,0:T(8,128)(2,1)S(1)} %collective-permute-done.2), channel_id=3, replica_groups=mesh['zl'=2,'y'=8,'x'=4,'zh'=4,'core'=2] {'core'}, dimensions={0}, use_global_device_ids=true | all-gather | bytes 786432 | tf_op jit(solution)/shard_map/all_gather | solution.py:257
  79.6 0.0 collective-permute-done.3
  79.6 2.2 %all-gather.2 = bf16[2048,128]{1,0:T(8,128)(2,1)S(1)} all-gather(bf16[1024,128]{1,0:T(8,128)(2,1)S(1)} %collective-permute-done.3), channel_id=4, replica_groups=mesh['zl'=2,'y'=8,'x'=4,'zh'=4,'core'=2] {'core'}, dimensions={0}, use_global_device_ids=true | all-gather | bytes 786432 | tf_op jit(solution)/shard_map/all_gather | solution.py:257
  81.8 0.0 collective-permute-done.4
  81.8 2.2 %all-gather.3 = bf16[2048,128]{1,0:T(8,128)(2,1)S(1)} all-gather(bf16[1024,128]{1,0:T(8,128)(2,1)S(1)} %collective-permute-done.4), channel_id=5, replica_groups=mesh['zl'=2,'y'=8,'x'=4,'zh'=4,'core'=2] {'core'}, dimensions={0}, use_global_device_ids=true | all-gather | bytes 786432 | tf_op jit(solution)/shard_map/all_gather | solution.py:257
  84.0 0.0 all-to-all-done.w_ref
  84.0 1.8 %project.1 = bf16[4,512,256]{2,1,0:T(8,128)(2,1)S(1)} custom-call(s32[2]{0:T(128)S(1)} %pad_add_fusion.place_ref, bf16[32,2,64,128]{3,2,1,0:T(8,128)(2,1)S(1)} %all-to-all-done.w_ref, bf16[2,1024,128]{2,1,0:T(8,128)(2,1)S(1)} %bitcast.14, bf16[2,1024,128]{2,1,0:T(8,128)(2,1)S(1)} %bitcast.15, bf16[2,1024,128]{2,1,0:T(8,128)(2,1)S(1)} %bitcast.16, ...), custom_call_target="tpu_custom_call" | custom-call | tf_op jit(solution)/shard_map/project/pallas_call | solution.py:206
  85.8 18.0 %all_to_all.20.parts_ref = bf16[4,512,256]{2,1,0:T(8,128)(2,1)S(1)} all-to-all(bf16[4,512,256]{2,1,0:T(8,128)(2,1)S(1)} %project.1), channel_id=1, replica_groups=mesh['zl'=2,'y'=8,'x'=4,'zh'=4,'core'=2] {'x'}, dimensions={0} | all-to-all | bytes 2097152 | tf_op jit(solution)/shard_map/all_to_all | solution.py:259
  103.9 0.8 finish.1
Async XLA Ops:
  0.0 46.4 %copy-start = (f32[512]{0:T(512)S(1)}, f32[512]{0:T(512)}, u32[]{:S(2)}) copy-start(f32[512]{0:T(512)} %param.13) | copy-start | bytes 6148
  2.0 5.0 %copy-start.1 = (bf16[512,64]{0,1:T(8,128)(2,1)S(1)}, bf16[512,64]{0,1:T(8,128)(2,1)}, u32[]{:S(2)}) copy-start(bf16[512,64]{0,1:T(8,128)(2,1)} %param.10) | copy-start | bytes 196612
  2.1 11.9 %all-to-all-start.1 = ((bf16[4,512,128]{2,1,0:T(8,128)(2,1)}), bf16[4,512,128]{2,1,0:T(8,128)(2,1)S(1)}, u32[]{:S(2)}, u32[]{:S(2)}) async-start(bf16[4,512,128]{2,1,0:T(8,128)(2,1)} %pack.1), calls=%async_computation.1 | async-start | bytes 1048576 | tf_op jit(solution)/shard_map/all_to_all | solution.py:245
  7.1 7.8 %collective-permute-start = (bf16[64,512]{1,0:T(8,128)(2,1)S(1)}, bf16[64,512]{1,0:T(8,128)(2,1)S(1)}, u32[]{:S(2)}, u32[]{:S(2)}) collective-permute-start(bf16[64,512]{1,0:T(8,128)(2,1)S(1)} %bitcast.18), channel_id=1, source_target_pairs={{0,0},{1,64},{2,128},{3,192},{4,256},{5,320},{6,384},{7,448},{32,3... | collective-permute-start | bytes 196616 | tf_op jit(solution)/shard_map/ppermute | solution.py:237
  15.5 21.8 %all-to-all-start.2 = ((f32[16,16,128]{2,1,0:T(8,128)}), f32[16,16,128]{2,1,0:T(8,128)S(1)}, u32[]{:S(2)}, u32[]{:S(2)}) async-start(f32[16,16,128]{2,1,0:T(8,128)} %sent.1), calls=%async_computation.2 | async-start | bytes 262144 | tf_op jit(solution)/shard_map/all_to_all | solution.py:250
  29.7 5.3 %collective-permute-start.1 = (bf16[64,512]{1,0:T(8,128)(2,1)S(1)}, bf16[64,512]{1,0:T(8,128)(2,1)S(1)}, u32[]{:S(2)}, u32[]{:S(2)}) collective-permute-start(bf16[64,512]{1,0:T(8,128)(2,1)S(1)} %collective-permute-done.own_ref.after_ref), channel_id=1, source_target_pairs={{0,256},{256,0},{1,257},{257,1},{2,258},{258,2},{3,259},{259,3},{4... | collective-permute-start | bytes 196616 | tf_op jit(solution)/shard_map/ppermute | solution.py:251
  37.3 46.7 %all-to-all-start = ((bf16[32,2,64,128]{3,2,1,0:T(8,128)(2,1)}), bf16[32,2,64,128]{3,2,1,0:T(8,128)(2,1)S(1)}, u32[]{:S(2)}, u32[]{:S(2)}) async-start(bf16[32,2,64,128]{3,2,1,0:T(8,128)(2,1)} %copies.1), calls=%async_computation | async-start | bytes 2097152 | tf_op jit(solution)/shard_map/all_to_all | solution.py:252
  48.3 19.5 %collective-permute-start.2 = (bf16[1024,128]{1,0:T(8,128)(2,1)S(1)}, bf16[1024,128]{1,0:T(8,128)(2,1)S(1)}, u32[]{:S(2)}, u32[]{:S(2)}) collective-permute-start(bf16[1024,128]{1,0:T(8,128)(2,1)S(1)} %scan.1), channel_id=1, source_target_pairs={{2,0},{4,2},{6,4},{0,6},{3,1},{5,3},{7,5},{1,7},{10,8},{12,10},{14... | collective-permute-start | bytes 786440 | tf_op jit(solution)/shard_map/ppermute | solution.py:255
  54.5 25.1 %collective-permute-start.3 = (bf16[1024,128]{1,0:T(8,128)(2,1)S(1)}, bf16[1024,128]{1,0:T(8,128)(2,1)S(1)}, u32[]{:S(2)}, u32[]{:S(2)}) collective-permute-start(bf16[1024,128]{1,0:T(8,128)(2,1)S(1)} %scan.1), channel_id=1, source_target_pairs={{4,0},{6,2},{0,4},{2,6},{5,1},{7,3},{1,5},{3,7},{12,8},{14,10},{8,... | collective-permute-start | bytes 786440 | tf_op jit(solution)/shard_map/ppermute | solution.py:255
  56.6 25.2 %collective-permute-start.4 = (bf16[1024,128]{1,0:T(8,128)(2,1)S(1)}, bf16[1024,128]{1,0:T(8,128)(2,1)S(1)}, u32[]{:S(2)}, u32[]{:S(2)}) collective-permute-start(bf16[1024,128]{1,0:T(8,128)(2,1)S(1)} %scan.1), channel_id=1, source_target_pairs={{6,0},{0,2},{2,4},{4,6},{7,1},{1,3},{3,5},{5,7},{14,8},{8,10},{10,... | collective-permute-start | bytes 786440 | tf_op jit(solution)/shard_map/ppermute | solution.py:255

commit v5 on v4

--- a/solution.py
+++ b/solution.py
@@ -13,6 +13,7 @@
 WIDE = 128
 BLOCK = 256
 VMEM = pltpu.CompilerParams(vmem_limit_bytes=40 * 1024 * 1024)
+DISTANCES = (0, 2, 3, 1)
 F32 = jnp.float32
 BF16 = jnp.bfloat16
 
@@ -183,7 +184,7 @@
         for part in range(2):
             tokens = slice(half * part, half * (part + 1))
             total = jnp.zeros((256, half), F32)
-            for d, g_ref in enumerate((g0_ref, g1_ref, g2_ref, g3_ref)):
+            for d, g_ref in zip(DISTANCES, (g0_ref, g1_ref, g2_ref, g3_ref)):
                 owner = lax.rem(zh + d, 4)
                 weights, values = [], []
                 for core in range(2):
@@ -252,7 +253,7 @@
     weight = lax.all_to_all(copies_of(own, far), ("y", "x"), 0, 0, tiled=True)
     gated = scan_call(me, moved, rate, amp, own_skip, ends, got)
     shifted = [gated] + [
-        lax.ppermute(gated, "zh", [((n + d) % 4, n) for n in range(4)]) for d in (1, 2, 3)
+        lax.ppermute(gated, "zh", [((n + d) % 4, n) for n in range(4)]) for d in DISTANCES[1:]
     ]
     both = [lax.all_gather(g, "core", axis=0, tiled=False) for g in shifted]
     parts = project(jnp.stack([zh, zl]), weight, *both)

time: 106 us -> 104 us (0.981)
  blocking collectives: 41.5 us -> 34.7 us
  waiting for transfers between devices: 4.29 us -> 8.36 us
  starting transfers between devices: 48.7 us -> 50 us
    all_gather x4, blocking collectives: 23.5 us -> 16.6 us  [per_device(): both = [lax.all_gather(g, 'core', axis=0, tiled=False) for g in shifted]]
    ppermute x3, waiting for transfers between devices: 0.01 us -> 4.07 us  [per_device(): lax.ppermute(gated, 'zh', [((n + d) % 4, n) for n in range(4)])]
    ppermute x3, starting transfers between devices: 12.1 us -> 13.3 us  [per_device(): lax.ppermute(gated, 'zh', [((n + d) % 4, n) for n in range(4)])]
  transfers between devices with their start and end apart: 8 -> 8, of which waited for: 3 -> 4; matrix products, arithmetic and copies ran while one was open for 1% -> 1% of each run, Pallas kernels for 4% -> 4%
where the time goes in v5:
time: 104 us; the launch traced here: 103 us
  starting transfers between devices  50 us (48%)
  blocking collectives  34.7 us (33%)
  Pallas kernels  9.09 us (9%)
  waiting for transfers between devices  8.36 us (8%)
    all_to_all x1, blocking collectives, per_device(): return finish(lax.all_to_all(parts, 'x', 0, 0, tiled=True))  18 us
    all_gather x4, blocking collectives, per_device(): both = [lax.all_gather(g, 'core', axis=0, tiled=False) for g in shifted]  16.6 us
    all_to_all x1, starting transfers between devices, per_device(): got = lax.all_to_all(sent_call(total, own), ('zl', 'y'), 0, 0, tiled=True)  14.2 us
    ppermute x3, starting transfers between devices, per_device(): lax.ppermute(gated, 'zh', [((n + d) % 4, n) for n in range(4)])  13.3 us
    all_to_all x1, starting transfers between devices, per_device(): weight = lax.all_to_all(copies_of(own, far), ('y', 'x'), 0, 0, tiled=True)  9.14 us
    ppermute x1, starting transfers between devices, place_weight(): return lax.ppermute(block, ('zl', 'y', 'zh', 'core'), perm)  5.05 us
    all_to_all x1, starting transfers between devices, per_device(): moved = lax.all_to_all(pack(q, k, v), 'x', 0, 0, tiled=True)  4.99 us
    ppermute x3, waiting for transfers between devices, per_device(): lax.ppermute(gated, 'zh', [((n + d) % 4, n) for n in range(4)])  4.07 us
  transfers between devices with their start and end apart: 8, of which 4 were waited for; matrix products, arithmetic and copies ran while one was open for 1% of the time, Pallas kernels for 4%

profile of v5, /device:TPU:1, one launch (start us, length us, event | category | flops | bytes accessed | tf_op | source)
XLA Modules:
  0.0 103.1 jit_solution(15789870925294253344)
XLA Ops:
  0.0 0.0 copy-start
  0.0 2.0 %pack.1 = bf16[4,512,128]{2,1,0:T(8,128)(2,1)} custom-call(bf16[512,256]{1,0:T(8,128)(2,1)} %q_hbm.1, bf16[512,256]{1,0:T(8,128)(2,1)} %k_hbm.1, bf16[512,256]{1,0:T(8,128)(2,1)} %v_hbm.1), custom_call_target="tpu_custom_call" | custom-call | tf_op jit(solution)/shard_map/pack/pallas_call | solution.py:42
  2.0 0.0 copy-start.1
  2.1 5.0 %all-to-all-start.1 = ((bf16[4,512,128]{2,1,0:T(8,128)(2,1)}), bf16[4,512,128]{2,1,0:T(8,128)(2,1)S(1)}, u32[]{:S(2)}, u32[]{:S(2)}) async-start(bf16[4,512,128]{2,1,0:T(8,128)(2,1)} %pack.1), calls=%async_computation.1 | async-start | bytes 1048576 | tf_op jit(solution)/shard_map/all_to_all | solution.py:246
  7.0 0.0 copy-done.1
  7.1 5.0 %collective-permute-start = (bf16[64,512]{1,0:T(8,128)(2,1)S(1)}, bf16[64,512]{1,0:T(8,128)(2,1)S(1)}, u32[]{:S(2)}, u32[]{:S(2)}) collective-permute-start(bf16[64,512]{1,0:T(8,128)(2,1)S(1)} %bitcast.18), channel_id=1, source_target_pairs={{0,0},{1,64},{2,128},{3,192},{4,256},{5,320},{6,384},{7,448},{32,3... | collective-permute-start | bytes 196616 | tf_op jit(solution)/shard_map/ppermute | solution.py:238
  12.1 0.7 multiply_bitcast_fusion
  12.8 1.1 %all-to-all-done.1.moved_ref = bf16[4,512,128]{2,1,0:T(8,128)(2,1)S(1)} async-done(((bf16[4,512,128]{2,1,0:T(8,128)(2,1)}), bf16[4,512,128]{2,1,0:T(8,128)(2,1)S(1)}, u32[]{:S(2)}, u32[]{:S(2)}) %all-to-all-start.1) | async-done | bytes 524320 | tf_op jit(solution)/shard_map/all_to_all | solution.py:246
  14.0 0.9 ends.1
  14.8 0.0 collective-permute-done.own_ref.after_ref
  14.9 0.7 sent.1
  15.5 14.2 %all-to-all-start.2 = ((f32[16,16,128]{2,1,0:T(8,128)}), f32[16,16,128]{2,1,0:T(8,128)S(1)}, u32[]{:S(2)}, u32[]{:S(2)}) async-start(f32[16,16,128]{2,1,0:T(8,128)} %sent.1), calls=%async_computation.2 | async-start | bytes 262144 | tf_op jit(solution)/shard_map/all_to_all | solution.py:251
  29.7 3.3 %collective-permute-start.1 = (bf16[64,512]{1,0:T(8,128)(2,1)S(1)}, bf16[64,512]{1,0:T(8,128)(2,1)S(1)}, u32[]{:S(2)}, u32[]{:S(2)}) collective-permute-start(bf16[64,512]{1,0:T(8,128)(2,1)S(1)} %collective-permute-done.own_ref.after_ref), channel_id=1, source_target_pairs={{0,256},{256,0},{1,257},{257,1},{2,258},{258,2},{3,259},{259,3},{4... | collective-permute-start | bytes 196616 | tf_op jit(solution)/shard_map/ppermute | solution.py:252
  33.0 2.0 %collective-permute-done.1.far_ref = bf16[64,512]{1,0:T(8,128)(2,1)S(1)} collective-permute-done((bf16[64,512]{1,0:T(8,128)(2,1)S(1)}, bf16[64,512]{1,0:T(8,128)(2,1)S(1)}, u32[]{:S(2)}, u32[]{:S(2)}) %collective-permute-start.1) | collective-permute-done | bytes 65568 | tf_op jit(solution)/shard_map/ppermute | solution.py:252
  35.0 1.1 %copies.1 = bf16[32,2,64,128]{3,2,1,0:T(8,128)(2,1)} custom-call(bf16[64,512]{1,0:T(8,128)(2,1)S(1)} %collective-permute-done.own_ref.after_ref, bf16[64,512]{1,0:T(8,128)(2,1)S(1)} %collective-permute-done.1.far_ref), custom_call_target="tpu_custom_call" | custom-call | tf_op jit(solution)/shard_map/copies/pallas_call | solution.py:172
  36.2 1.1 %all-to-all-done.2.got_ref = f32[16,16,128]{2,1,0:T(8,128)S(1)} async-done(((f32[16,16,128]{2,1,0:T(8,128)}), f32[16,16,128]{2,1,0:T(8,128)S(1)}, u32[]{:S(2)}, u32[]{:S(2)}) %all-to-all-start.2) | async-done | bytes 131104 | tf_op jit(solution)/shard_map/all_to_all | solution.py:251
  37.3 9.1 %all-to-all-start = ((bf16[32,2,64,128]{3,2,1,0:T(8,128)(2,1)}), bf16[32,2,64,128]{3,2,1,0:T(8,128)(2,1)S(1)}, u32[]{:S(2)}, u32[]{:S(2)}) async-start(bf16[32,2,64,128]{3,2,1,0:T(8,128)(2,1)} %copies.1), calls=%async_computation | async-start | bytes 2097152 | tf_op jit(solution)/shard_map/all_to_all | solution.py:253
  46.4 0.0 copy-done
  46.4 0.1 dynamic-slice_bitcast_fusion.skip_ref
  46.5 1.8 %scan.1 = bf16[1024,128]{1,0:T(8,128)(2,1)S(1)} custom-call(s32[1]{0:T(128)} %bitcast.3.me_ref, bf16[4,512,128]{2,1,0:T(8,128)(2,1)S(1)} %all-to-all-done.1.moved_ref, f32[16,128]{1,0:T(8,128)S(1)} %get-tuple-element.10.rate_ref, f32[16,128]{1,0:T(8,128)S(1)} %get-tuple-element.9.amp_ref, f32[1,128]{1,0:T(1,128)S(1)} %dynamic-slice_bitcast_fusion.skip_ref, ...), custom_call_target="tpu_custom_call" | custom-call | tf_op jit(solution)/shard_map/scan/pallas_call | solution.py:149
  48.3 5.9 %collective-permute-start.2 = (bf16[1024,128]{1,0:T(8,128)(2,1)S(1)}, bf16[1024,128]{1,0:T(8,128)(2,1)S(1)}, u32[]{:S(2)}, u32[]{:S(2)}) collective-permute-start(bf16[1024,128]{1,0:T(8,128)(2,1)S(1)} %scan.1), channel_id=1, source_target_pairs={{4,0},{6,2},{0,4},{2,6},{5,1},{7,3},{1,5},{3,7},{12,8},{14,10},{8,... | collective-permute-start | bytes 786440 | tf_op jit(solution)/shard_map/ppermute | solution.py:256
  54.2 0.1 pad_add_fusion.place_ref
  54.3 4.2 %collective-permute-start.3 = (bf16[1024,128]{1,0:T(8,128)(2,1)S(1)}, bf16[1024,128]{1,0:T(8,128)(2,1)S(1)}, u32[]{:S(2)}, u32[]{:S(2)}) collective-permute-start(bf16[1024,128]{1,0:T(8,128)(2,1)S(1)} %scan.1), channel_id=1, source_target_pairs={{6,0},{0,2},{2,4},{4,6},{7,1},{1,3},{3,5},{5,7},{14,8},{8,10},{10,... | collective-permute-start | bytes 786440 | tf_op jit(solution)/shard_map/ppermute | solution.py:256
  58.5 3.2 %collective-permute-start.4 = (bf16[1024,128]{1,0:T(8,128)(2,1)S(1)}, bf16[1024,128]{1,0:T(8,128)(2,1)S(1)}, u32[]{:S(2)}, u32[]{:S(2)}) collective-permute-start(bf16[1024,128]{1,0:T(8,128)(2,1)S(1)} %scan.1), channel_id=1, source_target_pairs={{2,0},{4,2},{6,4},{0,6},{3,1},{5,3},{7,5},{1,7},{10,8},{12,10},{14... | collective-permute-start | bytes 786440 | tf_op jit(solution)/shard_map/ppermute | solution.py:256
  61.7 7.3 %all-gather = bf16[2048,128]{1,0:T(8,128)(2,1)S(1)} all-gather(bf16[1024,128]{1,0:T(8,128)(2,1)S(1)} %scan.1), channel_id=2, replica_groups=mesh['zl'=2,'y'=8,'x'=4,'zh'=4,'core'=2] {'core'}, dimensions={0}, use_global_device_ids=true | all-gather | bytes 786432 | tf_op jit(solution)/shard_map/all_gather | solution.py:258
  69.0 0.0 collective-permute-done.2
  69.0 4.8 %all-gather.1 = bf16[2048,128]{1,0:T(8,128)(2,1)S(1)} all-gather(bf16[1024,128]{1,0:T(8,128)(2,1)S(1)} %collective-permute-done.2), channel_id=3, replica_groups=mesh['zl'=2,'y'=8,'x'=4,'zh'=4,'core'=2] {'core'}, dimensions={0}, use_global_device_ids=true | all-gather | bytes 786432 | tf_op jit(solution)/shard_map/all_gather | solution.py:258
  73.9 0.0 collective-permute-done.3
  73.9 2.2 %all-gather.2 = bf16[2048,128]{1,0:T(8,128)(2,1)S(1)} all-gather(bf16[1024,128]{1,0:T(8,128)(2,1)S(1)} %collective-permute-done.3), channel_id=4, replica_groups=mesh['zl'=2,'y'=8,'x'=4,'zh'=4,'core'=2] {'core'}, dimensions={0}, use_global_device_ids=true | all-gather | bytes 786432 | tf_op jit(solution)/shard_map/all_gather | solution.py:258
  76.0 4.1 %collective-permute-done.4 = bf16[1024,128]{1,0:T(8,128)(2,1)S(1)} collective-permute-done((bf16[1024,128]{1,0:T(8,128)(2,1)S(1)}, bf16[1024,128]{1,0:T(8,128)(2,1)S(1)}, u32[]{:S(2)}, u32[]{:S(2)}) %collective-permute-start.4) | collective-permute-done | bytes 262176 | tf_op jit(solution)/shard_map/ppermute | solution.py:256
  80.1 2.3 %all-gather.3 = bf16[2048,128]{1,0:T(8,128)(2,1)S(1)} all-gather(bf16[1024,128]{1,0:T(8,128)(2,1)S(1)} %collective-permute-done.4), channel_id=5, replica_groups=mesh['zl'=2,'y'=8,'x'=4,'zh'=4,'core'=2] {'core'}, dimensions={0}, use_global_device_ids=true | all-gather | bytes 786432 | tf_op jit(solution)/shard_map/all_gather | solution.py:258
  82.4 0.0 all-to-all-done.w_ref
  82.4 1.8 %project.1 = bf16[4,512,256]{2,1,0:T(8,128)(2,1)S(1)} custom-call(s32[2]{0:T(128)S(1)} %pad_add_fusion.place_ref, bf16[32,2,64,128]{3,2,1,0:T(8,128)(2,1)S(1)} %all-to-all-done.w_ref, bf16[2,1024,128]{2,1,0:T(8,128)(2,1)S(1)} %bitcast.14, bf16[2,1024,128]{2,1,0:T(8,128)(2,1)S(1)} %bitcast.15, bf16[2,1024,128]{2,1,0:T(8,128)(2,1)S(1)} %bitcast.16, ...), custom_call_target="tpu_custom_call" | custom-call | tf_op jit(solution)/shard_map/project/pallas_call | solution.py:207
  84.2 18.0 %all_to_all.20.parts_ref = bf16[4,512,256]{2,1,0:T(8,128)(2,1)S(1)} all-to-all(bf16[4,512,256]{2,1,0:T(8,128)(2,1)S(1)} %project.1), channel_id=1, replica_groups=mesh['zl'=2,'y'=8,'x'=4,'zh'=4,'core'=2] {'x'}, dimensions={0} | all-to-all | bytes 2097152 | tf_op jit(solution)/shard_map/all_to_all | solution.py:260
  102.3 0.8 finish.1
Async XLA Ops:
  0.0 46.4 %copy-start = (f32[512]{0:T(512)S(1)}, f32[512]{0:T(512)}, u32[]{:S(2)}) copy-start(f32[512]{0:T(512)} %param.13) | copy-start | bytes 6148
  2.0 5.0 %copy-start.1 = (bf16[512,64]{0,1:T(8,128)(2,1)S(1)}, bf16[512,64]{0,1:T(8,128)(2,1)}, u32[]{:S(2)}) copy-start(bf16[512,64]{0,1:T(8,128)(2,1)} %param.10) | copy-start | bytes 196612
  2.1 11.9 %all-to-all-start.1 = ((bf16[4,512,128]{2,1,0:T(8,128)(2,1)}), bf16[4,512,128]{2,1,0:T(8,128)(2,1)S(1)}, u32[]{:S(2)}, u32[]{:S(2)}) async-start(bf16[4,512,128]{2,1,0:T(8,128)(2,1)} %pack.1), calls=%async_computation.1 | async-start | bytes 1048576 | tf_op jit(solution)/shard_map/all_to_all | solution.py:246
  7.1 7.8 %collective-permute-start = (bf16[64,512]{1,0:T(8,128)(2,1)S(1)}, bf16[64,512]{1,0:T(8,128)(2,1)S(1)}, u32[]{:S(2)}, u32[]{:S(2)}) collective-permute-start(bf16[64,512]{1,0:T(8,128)(2,1)S(1)} %bitcast.18), channel_id=1, source_target_pairs={{0,0},{1,64},{2,128},{3,192},{4,256},{5,320},{6,384},{7,448},{32,3... | collective-permute-start | bytes 196616 | tf_op jit(solution)/shard_map/ppermute | solution.py:238
  15.5 21.8 %all-to-all-start.2 = ((f32[16,16,128]{2,1,0:T(8,128)}), f32[16,16,128]{2,1,0:T(8,128)S(1)}, u32[]{:S(2)}, u32[]{:S(2)}) async-start(f32[16,16,128]{2,1,0:T(8,128)} %sent.1), calls=%async_computation.2 | async-start | bytes 262144 | tf_op jit(solution)/shard_map/all_to_all | solution.py:251
  29.7 5.3 %collective-permute-start.1 = (bf16[64,512]{1,0:T(8,128)(2,1)S(1)}, bf16[64,512]{1,0:T(8,128)(2,1)S(1)}, u32[]{:S(2)}, u32[]{:S(2)}) collective-permute-start(bf16[64,512]{1,0:T(8,128)(2,1)S(1)} %collective-permute-done.own_ref.after_ref), channel_id=1, source_target_pairs={{0,256},{256,0},{1,257},{257,1},{2,258},{258,2},{3,259},{259,3},{4... | collective-permute-start | bytes 196616 | tf_op jit(solution)/shard_map/ppermute | solution.py:252
  37.3 45.1 %all-to-all-start = ((bf16[32,2,64,128]{3,2,1,0:T(8,128)(2,1)}), bf16[32,2,64,128]{3,2,1,0:T(8,128)(2,1)S(1)}, u32[]{:S(2)}, u32[]{:S(2)}) async-start(bf16[32,2,64,128]{3,2,1,0:T(8,128)(2,1)} %copies.1), calls=%async_computation | async-start | bytes 2097152 | tf_op jit(solution)/shard_map/all_to_all | solution.py:253
  48.3 20.7 %collective-permute-start.2 = (bf16[1024,128]{1,0:T(8,128)(2,1)S(1)}, bf16[1024,128]{1,0:T(8,128)(2,1)S(1)}, u32[]{:S(2)}, u32[]{:S(2)}) collective-permute-start(bf16[1024,128]{1,0:T(8,128)(2,1)S(1)} %scan.1), channel_id=1, source_target_pairs={{4,0},{6,2},{0,4},{2,6},{5,1},{7,3},{1,5},{3,7},{12,8},{14,10},{8,... | collective-permute-start | bytes 786440 | tf_op jit(solution)/shard_map/ppermute | solution.py:256
  54.3 19.6 %collective-permute-start.3 = (bf16[1024,128]{1,0:T(8,128)(2,1)S(1)}, bf16[1024,128]{1,0:T(8,128)(2,1)S(1)}, u32[]{:S(2)}, u32[]{:S(2)}) collective-permute-start(bf16[1024,128]{1,0:T(8,128)(2,1)S(1)} %scan.1), channel_id=1, source_target_pairs={{6,0},{0,2},{2,4},{4,6},{7,1},{1,3},{3,5},{5,7},{14,8},{8,10},{10,... | collective-permute-start | bytes 786440 | tf_op jit(solution)/shard_map/ppermute | solution.py:256
  58.5 21.6 %collective-permute-start.4 = (bf16[1024,128]{1,0:T(8,128)(2,1)S(1)}, bf16[1024,128]{1,0:T(8,128)(2,1)S(1)}, u32[]{:S(2)}, u32[]{:S(2)}) collective-permute-start(bf16[1024,128]{1,0:T(8,128)(2,1)S(1)} %scan.1), channel_id=1, source_target_pairs={{2,0},{4,2},{6,4},{0,6},{3,1},{5,3},{7,5},{1,7},{10,8},{12,10},{14... | collective-permute-start | bytes 786440 | tf_op jit(solution)/shard_map/ppermute | solution.py:256

commit v6 on v5

--- a/solution.py
+++ b/solution.py
@@ -165,7 +165,7 @@
         for j in range(4):
             piece = ref[:, WIDE * j : WIDE * (j + 1)]
             for y in range(8):
-                out_ref[4 * y + j, side] = piece
+                out_ref[8 * j + y, side] = piece
 
 
 def copies_of(own, far):
@@ -190,7 +190,7 @@
                 for core in range(2):
                     t = 2 * owner + core
                     place, side = 2 * lax.rem(t, 4) + h, lax.rem(t // 4 + zl, 2)
-                    weights.append(jnp.concatenate([w_ref[4 * place + n, side] for n in range(4)], axis=0))
+                    weights.append(jnp.concatenate([w_ref[8 * n + place, side] for n in range(4)], axis=0))
                     values.append(g_ref[core, tokens, :])
                 total += lax.dot_general(
                     jnp.concatenate(weights, axis=1),
@@ -250,7 +250,7 @@
     ends, total = ends_call(moved, rate)
     got = lax.all_to_all(sent_call(total, own), ("zl", "y"), 0, 0, tiled=True)
     far = lax.ppermute(own, "zl", [(0, 1), (1, 0)])
-    weight = lax.all_to_all(copies_of(own, far), ("y", "x"), 0, 0, tiled=True)
+    weight = lax.all_to_all(copies_of(own, far), ("x", "y"), 0, 0, tiled=True)
     gated = scan_call(me, moved, rate, amp, own_skip, ends, got)
     shifted = [gated] + [
         lax.ppermute(gated, "zh", [((n + d) % 4, n) for n in range(4)]) for d in DISTANCES[1:]

time: 104 us -> 104 us (level)
  no operation moved by 1% of the time
where the time goes in v6:
time: 104 us; the launch traced here: 103 us
  starting transfers between devices  50 us (48%)
  blocking collectives  34.7 us (33%)
  Pallas kernels  9.09 us (9%)
  waiting for transfers between devices  8.36 us (8%)
    all_to_all x1, blocking collectives, per_device(): return finish(lax.all_to_all(parts, 'x', 0, 0, tiled=True))  18 us
    all_gather x4, blocking collectives, per_device(): both = [lax.all_gather(g, 'core', axis=0, tiled=False) for g in shifted]  16.6 us
    all_to_all x1, starting transfers between devices, per_device(): got = lax.all_to_all(sent_call(total, own), ('zl', 'y'), 0, 0, tiled=True)  14.2 us
    ppermute x3, starting transfers between devices, per_device(): lax.ppermute(gated, 'zh', [((n + d) % 4, n) for n in range(4)])  13.3 us
    all_to_all x1, starting transfers between devices, per_device(): weight = lax.all_to_all(copies_of(own, far), ('x', 'y'), 0, 0, tiled=True)  9.14 us
    ppermute x1, starting transfers between devices, place_weight(): return lax.ppermute(block, ('zl', 'y', 'zh', 'core'), perm)  5.05 us
    all_to_all x1, starting transfers between devices, per_device(): moved = lax.all_to_all(pack(q, k, v), 'x', 0, 0, tiled=True)  4.99 us
    ppermute x3, waiting for transfers between devices, per_device(): lax.ppermute(gated, 'zh', [((n + d) % 4, n) for n in range(4)])  4.07 us
  transfers between devices with their start and end apart: 8, of which 4 were waited for; matrix products, arithmetic and copies ran while one was open for 1% of the time, Pallas kernels for 4%

profile of v6, /device:TPU:1, one launch (start us, length us, event | category | flops | bytes accessed | tf_op | source)
XLA Modules:
  0.0 103.1 jit_solution(206776551156178400)
XLA Ops:
  0.0 0.0 copy-start
  0.0 2.0 %pack.1 = bf16[4,512,128]{2,1,0:T(8,128)(2,1)} custom-call(bf16[512,256]{1,0:T(8,128)(2,1)} %q_hbm.1, bf16[512,256]{1,0:T(8,128)(2,1)} %k_hbm.1, bf16[512,256]{1,0:T(8,128)(2,1)} %v_hbm.1), custom_call_target="tpu_custom_call" | custom-call | tf_op jit(solution)/shard_map/pack/pallas_call | solution.py:42
  2.0 0.0 copy-start.1
  2.1 5.0 %all-to-all-start.1 = ((bf16[4,512,128]{2,1,0:T(8,128)(2,1)}), bf16[4,512,128]{2,1,0:T(8,128)(2,1)S(1)}, u32[]{:S(2)}, u32[]{:S(2)}) async-start(bf16[4,512,128]{2,1,0:T(8,128)(2,1)} %pack.1), calls=%async_computation.1 | async-start | bytes 1048576 | tf_op jit(solution)/shard_map/all_to_all | solution.py:246
  7.0 0.0 copy-done.1
  7.1 5.0 %collective-permute-start = (bf16[64,512]{1,0:T(8,128)(2,1)S(1)}, bf16[64,512]{1,0:T(8,128)(2,1)S(1)}, u32[]{:S(2)}, u32[]{:S(2)}) collective-permute-start(bf16[64,512]{1,0:T(8,128)(2,1)S(1)} %bitcast.18), channel_id=1, source_target_pairs={{0,0},{1,64},{2,128},{3,192},{4,256},{5,320},{6,384},{7,448},{32,3... | collective-permute-start | bytes 196616 | tf_op jit(solution)/shard_map/ppermute | solution.py:238
  12.1 0.7 multiply_bitcast_fusion
  12.8 1.1 %all-to-all-done.1.moved_ref = bf16[4,512,128]{2,1,0:T(8,128)(2,1)S(1)} async-done(((bf16[4,512,128]{2,1,0:T(8,128)(2,1)}), bf16[4,512,128]{2,1,0:T(8,128)(2,1)S(1)}, u32[]{:S(2)}, u32[]{:S(2)}) %all-to-all-start.1) | async-done | bytes 524320 | tf_op jit(solution)/shard_map/all_to_all | solution.py:246
  14.0 0.9 ends.1
  14.8 0.0 collective-permute-done.own_ref.after_ref
  14.9 0.7 sent.1
  15.5 14.2 %all-to-all-start.2 = ((f32[16,16,128]{2,1,0:T(8,128)}), f32[16,16,128]{2,1,0:T(8,128)S(1)}, u32[]{:S(2)}, u32[]{:S(2)}) async-start(f32[16,16,128]{2,1,0:T(8,128)} %sent.1), calls=%async_computation.2 | async-start | bytes 262144 | tf_op jit(solution)/shard_map/all_to_all | solution.py:251
  29.7 3.3 %collective-permute-start.1 = (bf16[64,512]{1,0:T(8,128)(2,1)S(1)}, bf16[64,512]{1,0:T(8,128)(2,1)S(1)}, u32[]{:S(2)}, u32[]{:S(2)}) collective-permute-start(bf16[64,512]{1,0:T(8,128)(2,1)S(1)} %collective-permute-done.own_ref.after_ref), channel_id=1, source_target_pairs={{0,256},{256,0},{1,257},{257,1},{2,258},{258,2},{3,259},{259,3},{4... | collective-permute-start | bytes 196616 | tf_op jit(solution)/shard_map/ppermute | solution.py:252
  33.0 2.0 %collective-permute-done.1.far_ref = bf16[64,512]{1,0:T(8,128)(2,1)S(1)} collective-permute-done((bf16[64,512]{1,0:T(8,128)(2,1)S(1)}, bf16[64,512]{1,0:T(8,128)(2,1)S(1)}, u32[]{:S(2)}, u32[]{:S(2)}) %collective-permute-start.1) | collective-permute-done | bytes 65568 | tf_op jit(solution)/shard_map/ppermute | solution.py:252
  35.0 1.1 %copies.1 = bf16[32,2,64,128]{3,2,1,0:T(8,128)(2,1)} custom-call(bf16[64,512]{1,0:T(8,128)(2,1)S(1)} %collective-permute-done.own_ref.after_ref, bf16[64,512]{1,0:T(8,128)(2,1)S(1)} %collective-permute-done.1.far_ref), custom_call_target="tpu_custom_call" | custom-call | tf_op jit(solution)/shard_map/copies/pallas_call | solution.py:172
  36.2 1.1 %all-to-all-done.2.got_ref = f32[16,16,128]{2,1,0:T(8,128)S(1)} async-done(((f32[16,16,128]{2,1,0:T(8,128)}), f32[16,16,128]{2,1,0:T(8,128)S(1)}, u32[]{:S(2)}, u32[]{:S(2)}) %all-to-all-start.2) | async-done | bytes 131104 | tf_op jit(solution)/shard_map/all_to_all | solution.py:251
  37.3 9.1 %all-to-all-start = ((bf16[32,2,64,128]{3,2,1,0:T(8,128)(2,1)}), bf16[32,2,64,128]{3,2,1,0:T(8,128)(2,1)S(1)}, u32[]{:S(2)}, u32[]{:S(2)}) async-start(bf16[32,2,64,128]{3,2,1,0:T(8,128)(2,1)} %copies.1), calls=%async_computation | async-start | bytes 2097152 | tf_op jit(solution)/shard_map/all_to_all | solution.py:253
  46.4 0.0 copy-done
  46.4 0.1 dynamic-slice_bitcast_fusion.skip_ref
  46.5 1.8 %scan.1 = bf16[1024,128]{1,0:T(8,128)(2,1)S(1)} custom-call(s32[1]{0:T(128)} %bitcast.3.me_ref, bf16[4,512,128]{2,1,0:T(8,128)(2,1)S(1)} %all-to-all-done.1.moved_ref, f32[16,128]{1,0:T(8,128)S(1)} %get-tuple-element.10.rate_ref, f32[16,128]{1,0:T(8,128)S(1)} %get-tuple-element.9.amp_ref, f32[1,128]{1,0:T(1,128)S(1)} %dynamic-slice_bitcast_fusion.skip_ref, ...), custom_call_target="tpu_custom_call" | custom-call | tf_op jit(solution)/shard_map/scan/pallas_call | solution.py:149
  48.3 5.9 %collective-permute-start.2 = (bf16[1024,128]{1,0:T(8,128)(2,1)S(1)}, bf16[1024,128]{1,0:T(8,128)(2,1)S(1)}, u32[]{:S(2)}, u32[]{:S(2)}) collective-permute-start(bf16[1024,128]{1,0:T(8,128)(2,1)S(1)} %scan.1), channel_id=1, source_target_pairs={{4,0},{6,2},{0,4},{2,6},{5,1},{7,3},{1,5},{3,7},{12,8},{14,10},{8,... | collective-permute-start | bytes 786440 | tf_op jit(solution)/shard_map/ppermute | solution.py:256
  54.2 0.1 pad_add_fusion.place_ref
  54.3 4.2 %collective-permute-start.3 = (bf16[1024,128]{1,0:T(8,128)(2,1)S(1)}, bf16[1024,128]{1,0:T(8,128)(2,1)S(1)}, u32[]{:S(2)}, u32[]{:S(2)}) collective-permute-start(bf16[1024,128]{1,0:T(8,128)(2,1)S(1)} %scan.1), channel_id=1, source_target_pairs={{6,0},{0,2},{2,4},{4,6},{7,1},{1,3},{3,5},{5,7},{14,8},{8,10},{10,... | collective-permute-start | bytes 786440 | tf_op jit(solution)/shard_map/ppermute | solution.py:256
  58.5 3.2 %collective-permute-start.4 = (bf16[1024,128]{1,0:T(8,128)(2,1)S(1)}, bf16[1024,128]{1,0:T(8,128)(2,1)S(1)}, u32[]{:S(2)}, u32[]{:S(2)}) collective-permute-start(bf16[1024,128]{1,0:T(8,128)(2,1)S(1)} %scan.1), channel_id=1, source_target_pairs={{2,0},{4,2},{6,4},{0,6},{3,1},{5,3},{7,5},{1,7},{10,8},{12,10},{14... | collective-permute-start | bytes 786440 | tf_op jit(solution)/shard_map/ppermute | solution.py:256
  61.7 7.3 %all-gather = bf16[2048,128]{1,0:T(8,128)(2,1)S(1)} all-gather(bf16[1024,128]{1,0:T(8,128)(2,1)S(1)} %scan.1), channel_id=2, replica_groups=mesh['zl'=2,'y'=8,'x'=4,'zh'=4,'core'=2] {'core'}, dimensions={0}, use_global_device_ids=true | all-gather | bytes 786432 | tf_op jit(solution)/shard_map/all_gather | solution.py:258
  69.0 0.0 collective-permute-done.2
  69.0 4.8 %all-gather.1 = bf16[2048,128]{1,0:T(8,128)(2,1)S(1)} all-gather(bf16[1024,128]{1,0:T(8,128)(2,1)S(1)} %collective-permute-done.2), channel_id=3, replica_groups=mesh['zl'=2,'y'=8,'x'=4,'zh'=4,'core'=2] {'core'}, dimensions={0}, use_global_device_ids=true | all-gather | bytes 786432 | tf_op jit(solution)/shard_map/all_gather | solution.py:258
  73.9 0.0 collective-permute-done.3
  73.9 2.2 %all-gather.2 = bf16[2048,128]{1,0:T(8,128)(2,1)S(1)} all-gather(bf16[1024,128]{1,0:T(8,128)(2,1)S(1)} %collective-permute-done.3), channel_id=4, replica_groups=mesh['zl'=2,'y'=8,'x'=4,'zh'=4,'core'=2] {'core'}, dimensions={0}, use_global_device_ids=true | all-gather | bytes 786432 | tf_op jit(solution)/shard_map/all_gather | solution.py:258
  76.0 4.1 %collective-permute-done.4 = bf16[1024,128]{1,0:T(8,128)(2,1)S(1)} collective-permute-done((bf16[1024,128]{1,0:T(8,128)(2,1)S(1)}, bf16[1024,128]{1,0:T(8,128)(2,1)S(1)}, u32[]{:S(2)}, u32[]{:S(2)}) %collective-permute-start.4) | collective-permute-done | bytes 262176 | tf_op jit(solution)/shard_map/ppermute | solution.py:256
  80.1 2.3 %all-gather.3 = bf16[2048,128]{1,0:T(8,128)(2,1)S(1)} all-gather(bf16[1024,128]{1,0:T(8,128)(2,1)S(1)} %collective-permute-done.4), channel_id=5, replica_groups=mesh['zl'=2,'y'=8,'x'=4,'zh'=4,'core'=2] {'core'}, dimensions={0}, use_global_device_ids=true | all-gather | bytes 786432 | tf_op jit(solution)/shard_map/all_gather | solution.py:258
  82.4 0.0 all-to-all-done.w_ref
  82.4 1.8 %project.1 = bf16[4,512,256]{2,1,0:T(8,128)(2,1)S(1)} custom-call(s32[2]{0:T(128)S(1)} %pad_add_fusion.place_ref, bf16[32,2,64,128]{3,2,1,0:T(8,128)(2,1)S(1)} %all-to-all-done.w_ref, bf16[2,1024,128]{2,1,0:T(8,128)(2,1)S(1)} %bitcast.14, bf16[2,1024,128]{2,1,0:T(8,128)(2,1)S(1)} %bitcast.15, bf16[2,1024,128]{2,1,0:T(8,128)(2,1)S(1)} %bitcast.16, ...), custom_call_target="tpu_custom_call" | custom-call | tf_op jit(solution)/shard_map/project/pallas_call | solution.py:207
  84.2 18.0 %all_to_all.20.parts_ref = bf16[4,512,256]{2,1,0:T(8,128)(2,1)S(1)} all-to-all(bf16[4,512,256]{2,1,0:T(8,128)(2,1)S(1)} %project.1), channel_id=1, replica_groups=mesh['zl'=2,'y'=8,'x'=4,'zh'=4,'core'=2] {'x'}, dimensions={0} | all-to-all | bytes 2097152 | tf_op jit(solution)/shard_map/all_to_all | solution.py:260
  102.3 0.8 finish.1
Async XLA Ops:
  0.0 46.4 %copy-start = (f32[512]{0:T(512)S(1)}, f32[512]{0:T(512)}, u32[]{:S(2)}) copy-start(f32[512]{0:T(512)} %param.13) | copy-start | bytes 6148
  2.0 5.0 %copy-start.1 = (bf16[512,64]{0,1:T(8,128)(2,1)S(1)}, bf16[512,64]{0,1:T(8,128)(2,1)}, u32[]{:S(2)}) copy-start(bf16[512,64]{0,1:T(8,128)(2,1)} %param.10) | copy-start | bytes 196612
  2.1 11.9 %all-to-all-start.1 = ((bf16[4,512,128]{2,1,0:T(8,128)(2,1)}), bf16[4,512,128]{2,1,0:T(8,128)(2,1)S(1)}, u32[]{:S(2)}, u32[]{:S(2)}) async-start(bf16[4,512,128]{2,1,0:T(8,128)(2,1)} %pack.1), calls=%async_computation.1 | async-start | bytes 1048576 | tf_op jit(solution)/shard_map/all_to_all | solution.py:246
  7.1 7.8 %collective-permute-start = (bf16[64,512]{1,0:T(8,128)(2,1)S(1)}, bf16[64,512]{1,0:T(8,128)(2,1)S(1)}, u32[]{:S(2)}, u32[]{:S(2)}) collective-permute-start(bf16[64,512]{1,0:T(8,128)(2,1)S(1)} %bitcast.18), channel_id=1, source_target_pairs={{0,0},{1,64},{2,128},{3,192},{4,256},{5,320},{6,384},{7,448},{32,3... | collective-permute-start | bytes 196616 | tf_op jit(solution)/shard_map/ppermute | solution.py:238
  15.5 21.8 %all-to-all-start.2 = ((f32[16,16,128]{2,1,0:T(8,128)}), f32[16,16,128]{2,1,0:T(8,128)S(1)}, u32[]{:S(2)}, u32[]{:S(2)}) async-start(f32[16,16,128]{2,1,0:T(8,128)} %sent.1), calls=%async_computation.2 | async-start | bytes 262144 | tf_op jit(solution)/shard_map/all_to_all | solution.py:251
  29.7 5.3 %collective-permute-start.1 = (bf16[64,512]{1,0:T(8,128)(2,1)S(1)}, bf16[64,512]{1,0:T(8,128)(2,1)S(1)}, u32[]{:S(2)}, u32[]{:S(2)}) collective-permute-start(bf16[64,512]{1,0:T(8,128)(2,1)S(1)} %collective-permute-done.own_ref.after_ref), channel_id=1, source_target_pairs={{0,256},{256,0},{1,257},{257,1},{2,258},{258,2},{3,259},{259,3},{4... | collective-permute-start | bytes 196616 | tf_op jit(solution)/shard_map/ppermute | solution.py:252
  37.3 45.1 %all-to-all-start = ((bf16[32,2,64,128]{3,2,1,0:T(8,128)(2,1)}), bf16[32,2,64,128]{3,2,1,0:T(8,128)(2,1)S(1)}, u32[]{:S(2)}, u32[]{:S(2)}) async-start(bf16[32,2,64,128]{3,2,1,0:T(8,128)(2,1)} %copies.1), calls=%async_computation | async-start | bytes 2097152 | tf_op jit(solution)/shard_map/all_to_all | solution.py:253
  48.3 20.7 %collective-permute-start.2 = (bf16[1024,128]{1,0:T(8,128)(2,1)S(1)}, bf16[1024,128]{1,0:T(8,128)(2,1)S(1)}, u32[]{:S(2)}, u32[]{:S(2)}) collective-permute-start(bf16[1024,128]{1,0:T(8,128)(2,1)S(1)} %scan.1), channel_id=1, source_target_pairs={{4,0},{6,2},{0,4},{2,6},{5,1},{7,3},{1,5},{3,7},{12,8},{14,10},{8,... | collective-permute-start | bytes 786440 | tf_op jit(solution)/shard_map/ppermute | solution.py:256
  54.3 19.6 %collective-permute-start.3 = (bf16[1024,128]{1,0:T(8,128)(2,1)S(1)}, bf16[1024,128]{1,0:T(8,128)(2,1)S(1)}, u32[]{:S(2)}, u32[]{:S(2)}) collective-permute-start(bf16[1024,128]{1,0:T(8,128)(2,1)S(1)} %scan.1), channel_id=1, source_target_pairs={{6,0},{0,2},{2,4},{4,6},{7,1},{1,3},{3,5},{5,7},{14,8},{8,10},{10,... | collective-permute-start | bytes 786440 | tf_op jit(solution)/shard_map/ppermute | solution.py:256
  58.5 21.6 %collective-permute-start.4 = (bf16[1024,128]{1,0:T(8,128)(2,1)S(1)}, bf16[1024,128]{1,0:T(8,128)(2,1)S(1)}, u32[]{:S(2)}, u32[]{:S(2)}) collective-permute-start(bf16[1024,128]{1,0:T(8,128)(2,1)S(1)} %scan.1), channel_id=1, source_target_pairs={{2,0},{4,2},{6,4},{0,6},{3,1},{5,3},{7,5},{1,7},{10,8},{12,10},{14... | collective-permute-start | bytes 786440 | tf_op jit(solution)/shard_map/ppermute | solution.py:256
